TPU v7x, 512 devices: a whole 4x8x8 slice. The times are simulated.
512 devices in a mesh: ens: 2 (over core), lat: 32 (over z, x), chan: 8 (over y).
Axes of the slice: x: 4, y: 8, z: 8, core: 2. Of those that a mesh axis runs over, the one named last changes fastest.
Arguments:
- field: bfloat16 [2, 384, 128, 256], P('ens', 'chan', 'lat'), may hold values from -6 to 6
- cotangent: bfloat16 [2, 384, 128, 256], P('ens', 'chan', 'lat'), may hold values from -6 to 6
- spec_weight: float32 [2, 64, 384], P(None, None, 'chan'), may hold values from -8 to 8
- disco_coef: float32 [128, 9], replicated, may hold values from -2 to 2
- disco_weight: float32 [9, 384], P(None, 'chan'), may hold values from -5 to 5
- disco_rows: int32 [128, 9], replicated, may hold values from 0 to 127, as said below
- disco_shift: int32 [128, 9], replicated, may hold values from -8 to 8
- w_hidden: bfloat16 [384, 768], replicated, may hold values from -0.3125 to 0.3125
- w_output: bfloat16 [768, 384], replicated, may hold values from -0.21875 to 0.21875
Outputs:
- grad_field: bfloat16 [2, 384, 128, 256], P('ens', 'chan', 'lat')
- grad_spec_weight: float32 [2, 64, 384], P(None, None, 'chan')
- grad_disco_weight: float32 [9, 384], P(None, 'chan')
- grad_w_hidden: float32 [384, 768], P('lat')
- grad_w_output: float32 [768, 384], P('lat')
Inputs may be any that keep to these rules, and one draw needn't show every extreme that they name: Entry k of row i of disco_rows names a latitude row within 2 rows of i.
All inputs are finite; a program needn't handle non-finite values.
Results may differ from a plain program's by a relative error of at most 0.013.
Values may be sent and summed in bfloat16 or wider, within the bound.
A program may use at most 64 MiB of HBM per device.

v0:
```python
import math

import jax
import jax.numpy as jnp
from jax import lax
from jax.sharding import PartitionSpec as P

HALO = 2
SHIFT = 8


norm_eps = 1e-06
inv_root_two = 0.7071067811865476
inv_root_tau = 0.3989422804014327
highest = lax.Precision.HIGHEST


def padded_2(block, sides, width):
    for axis, dim in sides:
        count = lax.axis_size(axis)
        forward = [(i, i + 1) for i in range(count - 1)]
        backward = [(target, source) for source, target in forward]
        low = lax.ppermute(
            lax.slice_in_dim(block, block.shape[dim] - width, None, axis=dim), axis, forward
        )
        high = lax.ppermute(lax.slice_in_dim(block, 0, width, axis=dim), axis, backward)
        block = jnp.concatenate([low, block, high], axis=dim)
    return block


def colatitudes(lat_count):
    return (jnp.arange(lat_count, dtype=jnp.int32).astype(jnp.float32) + 0.5) * (
        math.pi / lat_count
    )


def legendre_rows(first_order, order_count, lat_count, degree_count):
    colatitude = colatitudes(lat_count)
    cosine = jnp.cos(colatitude)
    sine_rows = jnp.sin(colatitude)
    orders = (first_order + jnp.arange(order_count, dtype=jnp.int32)).astype(jnp.float32)
    log_start = 0.5 * (
        jnp.log((2.0 * orders + 1.0) / (4.0 * math.pi))
        + lax.lgamma(orders + 0.5)
        - lax.lgamma(orders + 1.0)
        - 0.5 * math.log(math.pi)
    )
    diagonal = jnp.exp(log_start[:, None] + orders[:, None] * jnp.log(sine_rows)[None, :])

    def advance(carry, degree):
        previous, before = carry
        degree_value = degree.astype(jnp.float32)
        above = degree_value > orders
        upper_term = jnp.where(above, 4.0 * degree_value * degree_value - 1.0, 1.0)
        lower_term = jnp.where(above, degree_value * degree_value - orders * orders, 1.0)
        factor = jnp.sqrt(upper_term / lower_term)
        behind = jnp.where(
            above, (degree_value - 1.0) * (degree_value - 1.0) - orders * orders, 0.0
        )
        damping = jnp.sqrt(behind / (4.0 * (degree_value - 1.0) * (degree_value - 1.0) - 1.0))
        recurred = factor[:, None] * (cosine[None, :] * previous - damping[:, None] * before)
        current = jnp.where(
            above[:, None], recurred, jnp.where((degree_value == orders)[:, None], diagonal, 0.0)
        )
        return ((current, previous), current)

    zero_rows = jnp.zeros((order_count, lat_count), jnp.float32)
    finish, stacked = lax.scan(
        advance, (zero_rows, zero_rows), jnp.arange(degree_count, dtype=jnp.int32), unroll=True
    )
    return jnp.transpose(stacked, (1, 0, 2))


def quadrature(lat_count, lon_count):
    return 2.0 * math.pi / lon_count * (math.pi / lat_count) * jnp.sin(colatitudes(lat_count))


def lon_tables(lon_count, mode_count):
    columns = jnp.arange(lon_count, dtype=jnp.int32)
    mode_ids = jnp.arange(mode_count, dtype=jnp.int32)
    phase_ids = columns[:, None] * mode_ids[None, :] % lon_count
    angles = phase_ids.astype(jnp.float32) * (2.0 * math.pi / lon_count)
    cosine = jnp.cos(angles)
    sine_part = jnp.sin(angles)
    forward = jnp.concatenate([cosine, -sine_part], axis=1).astype(jnp.bfloat16)
    doubled = jnp.where(mode_ids == 0, 1.0, 2.0).astype(jnp.float32)[None, :]
    inverse = jnp.transpose(
        jnp.concatenate([doubled * cosine, -doubled * sine_part], axis=1)
    ).astype(jnp.bfloat16)
    return (forward, inverse)


def apply_filter(coeffs, spec_weight):
    real_weight = jnp.transpose(spec_weight[0])[:, None, :]
    imag_weight = jnp.transpose(spec_weight[1])[:, None, :]
    real_part = coeffs[:, 0]
    imag_part = coeffs[:, 1]
    return jnp.stack(
        [
            real_weight * real_part - imag_weight * imag_part,
            real_weight * imag_part + imag_weight * real_part,
        ],
        axis=1,
    )


def filter_adjoint(grads, coeffs, spec_weight):
    real_weight = jnp.transpose(spec_weight[0])[:, None, :]
    imag_weight = jnp.transpose(spec_weight[1])[:, None, :]
    grad_real = grads[:, 0]
    grad_imag = grads[:, 1]
    real_part = coeffs[:, 0]
    imag_part = coeffs[:, 1]
    weight_zero = jnp.transpose(jnp.sum(grad_real * real_part + grad_imag * imag_part, axis=1))
    weight_one = jnp.transpose(jnp.sum(grad_imag * real_part - grad_real * imag_part, axis=1))
    adjoint_coeffs = jnp.stack(
        [
            real_weight * grad_real + imag_weight * grad_imag,
            real_weight * grad_imag - imag_weight * grad_real,
        ],
        axis=1,
    )
    return (adjoint_coeffs, jnp.stack([weight_zero, weight_one], axis=0))


def mlp_backward(mixed_rows, adjoint_rows, w_hidden, w_output):
    mixed32 = mixed_rows.astype(jnp.float32)
    rscale = lax.rsqrt(jnp.mean(mixed32 * mixed32, axis=0, keepdims=True) + norm_eps)
    normed32 = mixed32 * rscale
    normed = normed32.astype(jnp.bfloat16)
    preact = lax.dot_general(
        w_hidden, normed, (((0,), (0,)), ((), ())), preferred_element_type=jnp.float32
    )
    activated = jax.nn.gelu(preact, approximate=False).astype(jnp.bfloat16)
    grad_output = lax.dot_general(
        activated, adjoint_rows, (((1,), (1,)), ((), ())), preferred_element_type=jnp.float32
    )
    grad_act = lax.dot_general(
        w_output, adjoint_rows, (((1,), (0,)), ((), ())), preferred_element_type=jnp.float32
    )
    cumulative = 0.5 * (1.0 + lax.erf(preact * inv_root_two))
    density = jnp.exp(-0.5 * preact * preact) * inv_root_tau
    grad_pre = (grad_act * (cumulative + preact * density)).astype(jnp.bfloat16)
    grad_hidden = lax.dot_general(
        normed, grad_pre, (((1,), (1,)), ((), ())), preferred_element_type=jnp.float32
    )
    grad_normed = lax.dot_general(
        w_hidden, grad_pre, (((1,), (0,)), ((), ())), preferred_element_type=jnp.float32
    )
    grad_mixed = (
        rscale * (grad_normed - normed32 * jnp.mean(grad_normed * normed32, axis=0, keepdims=True))
    ).astype(jnp.bfloat16)
    return (grad_mixed, grad_hidden, grad_output)


def to_modes(spectrum):
    return lax.all_to_all(spectrum, "lat", split_axis=3, concat_axis=1, tiled=True)


def to_bands(spectrum):
    return lax.all_to_all(spectrum, "lat", split_axis=1, concat_axis=3, tiled=True)


def wrap_lon(values, width):
    return jnp.concatenate([values[:, :, -width:], values, values[:, :, :width]], axis=2)


def disco_kernel(rows_tab, shift_tab, coef_tab, centre, disco_weight):
    row_step = rows_tab - centre[:, None] + HALO
    lon_step = shift_tab + SHIFT
    reach = jnp.arange(2 * HALO + 1, dtype=jnp.int32)
    span = jnp.arange(2 * SHIFT + 1, dtype=jnp.int32)
    onehot = (
        (row_step[:, :, None, None] == reach[None, None, :, None])
        & (lon_step[:, :, None, None] == span[None, None, None, :])
    ).astype(jnp.float32)
    kernel = jnp.einsum("rk,rkpq,kc->crpq", coef_tab, onehot, disco_weight, precision=highest)
    return (onehot, kernel)


def shards(
    field,
    cotangent,
    spec_weight,
    disco_coef,
    disco_weight,
    disco_rows,
    disco_shift,
    w_hidden,
    w_output,
):
    member = field[0]
    adjoint_member = cotangent[0]
    channels, lat_rows, lon_count = member.shape
    band_count = lax.axis_size("lat")
    lat_count = lat_rows * band_count
    mode_count = lat_count // 2
    modes_here = mode_count // band_count
    band_index = lax.axis_index("lat")
    first_row = band_index * lat_rows
    forward, inverse = lon_tables(lon_count, mode_count)
    legendre = legendre_rows(band_index * modes_here, modes_here, lat_count, mode_count)
    weighted = legendre * quadrature(lat_count, lon_count)[None, None, :]
    grad_scale = 1.0 / math.sqrt(lax.axis_size("ens") * lat_count * lon_count)
    reach_count = 2 * HALO + 1
    span_count = 2 * SHIFT + 1
    adjoint_rows = lax.all_to_all(adjoint_member, "chan", split_axis=2, concat_axis=0, tiled=True)
    spectrum = jnp.dot(
        member.reshape(channels * lat_rows, lon_count), forward, preferred_element_type=jnp.float32
    )
    spectrum = spectrum.astype(jnp.bfloat16).reshape(channels, lat_rows, 2, mode_count)
    mode_block = to_modes(spectrum)
    coeffs = jnp.einsum(
        "citm,mli->ctml", mode_block.astype(jnp.float32), weighted, precision=highest
    )
    synthesis = jnp.einsum(
        "ctml,mli->citm", apply_filter(coeffs, spec_weight), legendre, precision=highest
    ).astype(jnp.bfloat16)
    band_block = to_bands(synthesis)
    spectral = jnp.dot(
        band_block.reshape(channels * lat_rows, 2 * mode_count),
        inverse,
        preferred_element_type=jnp.float32,
    )
    spectral = spectral.reshape(channels, lat_rows, lon_count)
    global_rows = first_row + jnp.arange(lat_rows, dtype=jnp.int32)
    rows_here = lax.dynamic_slice_in_dim(disco_rows, first_row, lat_rows, 0)
    shift_here = lax.dynamic_slice_in_dim(disco_shift, first_row, lat_rows, 0)
    coef_here = lax.dynamic_slice_in_dim(disco_coef, first_row, lat_rows, 0)
    onehot_here, kernel_here = disco_kernel(
        rows_here, shift_here, coef_here, global_rows, disco_weight
    )
    padded = padded_2(member, (("lat", 1),), HALO)
    wide_field = wrap_lon(padded, SHIFT)
    disco_out = jnp.zeros((channels, lat_rows, lon_count), jnp.float32)
    for reach in range(reach_count):
        for span in range(span_count):
            window = wide_field[:, reach : reach + lat_rows, span : span + lon_count].astype(
                jnp.float32
            )
            disco_out = disco_out + kernel_here[:, :, reach, span][:, :, None] * window
    mixed_field = (spectral + disco_out).astype(jnp.bfloat16)
    mixed_rows = lax.all_to_all(mixed_field, "chan", split_axis=2, concat_axis=0, tiled=True)
    all_channels = mixed_rows.shape[0]
    row_width = mixed_rows.shape[2]
    grad_rows, grad_hidden, grad_output = mlp_backward(
        mixed_rows.reshape(all_channels, lat_rows * row_width),
        adjoint_rows.reshape(all_channels, lat_rows * row_width),
        w_hidden,
        w_output,
    )
    grad_field = lax.all_to_all(
        grad_rows.reshape(all_channels, lat_rows, row_width),
        "chan",
        split_axis=0,
        concat_axis=2,
        tiled=True,
    )
    grad_synth = lax.dot_general(
        grad_field.reshape(channels * lat_rows, lon_count),
        inverse,
        (((1,), (1,)), ((), ())),
        preferred_element_type=jnp.float32,
    )
    grad_synth = grad_synth.astype(jnp.bfloat16).reshape(channels, lat_rows, 2, mode_count)
    grad_modes = to_modes(grad_synth)
    grad_filtered = jnp.einsum(
        "citm,mli->ctml", grad_modes.astype(jnp.float32), legendre, precision=highest
    )
    grad_coeffs, filter_part = filter_adjoint(grad_filtered, coeffs, spec_weight)
    grad_spectrum = jnp.einsum("ctml,mli->citm", grad_coeffs, weighted, precision=highest).astype(
        jnp.bfloat16
    )
    grad_lines = to_bands(grad_spectrum)
    spectral_back = lax.dot_general(
        grad_lines.reshape(channels * lat_rows, 2 * mode_count),
        forward,
        (((1,), (1,)), ((), ())),
        preferred_element_type=jnp.float32,
    )
    spectral_back = spectral_back.reshape(channels, lat_rows, lon_count)
    grad_wide = grad_field.astype(jnp.float32)
    reach_sums = []
    for reach in range(reach_count):
        span_sums = []
        for span in range(span_count):
            window = wide_field[:, reach : reach + lat_rows, span : span + lon_count].astype(
                jnp.float32
            )
            span_sums.append(jnp.sum(window * grad_wide, axis=2))
        reach_sums.append(jnp.stack(span_sums, axis=2))
    inner_sum = jnp.stack(reach_sums, axis=2)
    disco_part = jnp.einsum(
        "ik,ikpq,cipq->kc", coef_here, onehot_here, inner_sum, precision=highest
    )
    rimmed = padded_2(grad_field, (("lat", 1),), HALO)
    wide_grads = wrap_lon(rimmed, SHIFT)
    ext_count = lat_rows + 2 * HALO
    ext_rows = first_row - HALO + jnp.arange(ext_count, dtype=jnp.int32)
    rows_ext = lax.dynamic_slice_in_dim(
        jnp.pad(disco_rows, ((HALO, HALO), (0, 0))), first_row, ext_count, 0
    )
    shift_ext = lax.dynamic_slice_in_dim(
        jnp.pad(disco_shift, ((HALO, HALO), (0, 0))), first_row, ext_count, 0
    )
    coef_ext = lax.dynamic_slice_in_dim(
        jnp.pad(disco_coef, ((HALO, HALO), (0, 0))), first_row, ext_count, 0
    )
    onehot_ext, kernel_ext = disco_kernel(rows_ext, shift_ext, coef_ext, ext_rows, disco_weight)
    spread = jnp.zeros((channels, lat_rows, lon_count), jnp.float32)
    for reach in range(reach_count):
        row_start = 2 * HALO - reach
        for span in range(span_count):
            col_start = 2 * SHIFT - span
            window = wide_grads[
                :, row_start : row_start + lat_rows, col_start : col_start + lon_count
            ].astype(jnp.float32)
            spread = (
                spread
                + kernel_ext[:, row_start : row_start + lat_rows, reach, span][:, :, None] * window
            )
    grad_input = (adjoint_member.astype(jnp.float32) + spectral_back + spread).astype(jnp.bfloat16)
    filter_total, disco_total = lax.psum((filter_part, disco_part), ("ens", "lat"))
    total_hidden, total_output = lax.psum((grad_hidden, grad_output), ("ens", "lat", "chan"))
    hidden_rows = total_hidden.shape[0] // band_count
    output_rows = total_output.shape[0] // band_count
    share_hidden = lax.dynamic_slice_in_dim(total_hidden, band_index * hidden_rows, hidden_rows, 0)
    share_output = lax.dynamic_slice_in_dim(total_output, band_index * output_rows, output_rows, 0)
    return (
        grad_input[None],
        filter_total,
        disco_total * grad_scale,
        share_hidden * grad_scale,
        share_output * grad_scale,
    )


def solution(mesh):
    in_specs = (
        P("ens", "chan", "lat", None),
        P("ens", "chan", "lat", None),
        P(None, None, "chan"),
        P(),
        P(None, "chan"),
        P(),
        P(),
        P(),
        P(),
    )
    out_specs = (
        P("ens", "chan", "lat", None),
        P(None, None, "chan"),
        P(None, "chan"),
        P("lat", None),
        P("lat", None),
    )
    return jax.shard_map(shards, mesh=mesh, in_specs=in_specs, out_specs=out_specs, check_vma=False)
```

profile of v0, /device:TPU:256, one launch (start us, length us, event | category | flops | bytes accessed | tf_op | source)
XLA Modules:
  0.0 485.7 jit_solution(5748793667730272015)
XLA Ops:
  9.7 9.9 %all-to-all-start = ((bf16[32,2,384]{2,1,0:T(2,128)(2,1)}), bf16[32,2,384]{2,1,0:T(2,128)(2,1)S(1)}, u32[]{:S(2)}, u32[]{:S(2)}) async-start(bf16[32,2,384]{2,1,0:T(2,128)(2,1)} %reshape.55196), calls=%async_computation | async-start | bytes 98304 | tf_op jit(solution)/shard_map/all_to_all | solution.py:157
  19.6 3.4 collective-permute-start
  23.0 5.8 %collective-permute-start.1 = (bf16[48,2,256]{2,0,1:T(8,128)(2,1)S(1)}, bf16[48,2,256]{2,0,1:T(8,128)(2,1)S(1)}, u32[]{:S(2)}, u32[]{:S(2)}) collective-permute-start(bf16[48,2,256]{2,0,1:T(8,128)(2,1)S(1)} %get-tuple-element.536), channel_id=1, source_target_pairs={{8,0},{16,8},{24,16},{32,24},{40,32},{48,40},{56,48},{64,56},{72,6... | collective-permute-start | bytes 147464 | tf_op jit(solution)/shard_map/ppermute | solution.py:26
  89.2 7.4 %all-to-all-start.1 = ((bf16[32,2,384]{2,1,0:T(2,128)(2,1)}), bf16[32,2,384]{2,1,0:T(2,128)(2,1)S(1)}, u32[]{:S(2)}, u32[]{:S(2)}) async-start(bf16[32,2,384]{2,1,0:T(2,128)(2,1)} %reshape.55198), calls=%async_computation.1 | async-start | bytes 98304 | tf_op jit(solution)/shard_map/all_to_all | solution.py:161
  96.8 4.9 %all-to-all-done.1 = bf16[32,2,384]{2,1,0:T(2,128)(2,1)S(1)} async-done(((bf16[32,2,384]{2,1,0:T(2,128)(2,1)}), bf16[32,2,384]{2,1,0:T(2,128)(2,1)S(1)}, u32[]{:S(2)}, u32[]{:S(2)}) %all-to-all-start.1) | async-done | bytes 49184 | tf_op jit(solution)/shard_map/all_to_all | solution.py:161
  101.7 7.1 %all-to-all-start.3 = ((bf16[8,2,3072]{2,1,0:T(2,128)(2,1)}), bf16[8,2,3072]{2,1,0:T(2,128)(2,1)S(1)}, u32[]{:S(2)}, u32[]{:S(2)}) async-start(bf16[8,2,3072]{2,1,0:T(2,128)(2,1)} %reshape.55202), calls=%async_computation.3 | async-start | bytes 196608 | tf_op jit(solution)/shard_map/all_to_all | solution.py:207
  109.5 6.0 %fusion.2 = bf16[48,4,256]{2,0,1:T(8,128)(2,1)S(1)} fusion(bf16[48,4,128]{0,2,1:T(8,128)(2,1)S(1)} %bitcast.623, bf16[48,4,256]{2,0,1:T(8,128)(2,1)S(1)} %bitcast.596, f32[48,4]{0,1:T(4,128)S(1)} %bitcast.820, f32[48,4]{0,1:T(4,128)S(1)} %bitcast.821, f32[48,4]{0,1:T(4,128)S(1)} %bitcast.822, f32[48,4]{0,1:T(4,128)S(1)} %bitcast.823, ...), kind=kOutput, calls=%fused_computation.173 | convolution fusion | flops 25493504 | bytes 8339200 | tf_op jit(solution)/shard_map/dot_general | solution.py:220
  117.6 6.4 %all-to-all-start.2 = ((bf16[8,2,3072]{2,1,0:T(2,128)(2,1)}), bf16[8,2,3072]{2,1,0:T(2,128)(2,1)S(1)}, u32[]{:S(2)}, u32[]{:S(2)}) async-start(bf16[8,2,3072]{2,1,0:T(2,128)(2,1)} %reshape.55200), calls=%async_computation.2 | async-start | bytes 196608 | tf_op jit(solution)/shard_map/all_to_all | solution.py:243
  125.2 7.5 %all-to-all-done.2 = bf16[8,2,3072]{2,1,0:T(2,128)(2,1)S(1)} async-done(((bf16[8,2,3072]{2,1,0:T(2,128)(2,1)}), bf16[8,2,3072]{2,1,0:T(2,128)(2,1)S(1)}, u32[]{:S(2)}, u32[]{:S(2)}) %all-to-all-start.2) | async-done | bytes 98336 | tf_op jit(solution)/shard_map/all_to_all | solution.py:243
  134.6 2.0 fusion.24
  138.8 3.4 all-to-all-start.4
  142.5 1.5 fusion.613
  144.0 6.9 %all-to-all-done.4 = bf16[8,2,3072]{2,1,0:T(2,128)(2,1)S(1)} async-done(((bf16[8,2,3072]{2,1,0:T(2,128)(2,1)}), bf16[8,2,3072]{2,1,0:T(2,128)(2,1)S(1)}, u32[]{:S(2)}, u32[]{:S(2)}) %all-to-all-start.4) | async-done | bytes 98336 | tf_op jit(solution)/shard_map/all_to_all | solution.py:252
  152.1 1.1 fusion.210
  153.2 1.2 fusion.219
  155.5 1.2 fusion.218
  158.3 8.6 %all-to-all-start.5 = ((bf16[32,2,384]{2,1,0:T(2,128)(2,1)}), bf16[32,2,384]{2,1,0:T(2,128)(2,1)S(1)}, u32[]{:S(2)}, u32[]{:S(2)}) async-start(bf16[32,2,384]{2,1,0:T(2,128)(2,1)} %reshape.55206), calls=%async_computation.5 | async-start | bytes 98304 | tf_op jit(solution)/shard_map/all_to_all | solution.py:157
  166.9 3.4 collective-permute-start.2
  170.3 5.8 %collective-permute-start.3 = (bf16[48,2,256]{2,0,1:T(8,128)(2,1)S(1)}, bf16[48,2,256]{2,0,1:T(8,128)(2,1)S(1)}, u32[]{:S(2)}, u32[]{:S(2)}) collective-permute-start(bf16[48,2,256]{2,0,1:T(8,128)(2,1)S(1)} %get-tuple-element.534), channel_id=1, source_target_pairs={{8,0},{16,8},{24,16},{32,24},{40,32},{48,40},{56,48},{64,56},{72,6... | collective-permute-start | bytes 147464 | tf_op jit(solution)/shard_map/ppermute | solution.py:26
  180.3 10.2 %all-to-all-start.6 = ((bf16[32,2,384]{2,1,0:T(2,128)(2,1)}), bf16[32,2,384]{2,1,0:T(2,128)(2,1)S(1)}, u32[]{:S(2)}, u32[]{:S(2)}) async-start(bf16[32,2,384]{2,1,0:T(2,128)(2,1)} %reshape.55208), calls=%async_computation.6 | async-start | bytes 98304 | tf_op jit(solution)/shard_map/all_to_all | solution.py:161
  190.5 276.9 %all-reduce.4 = (f32[2,64,48]{1,2,0:T(8,128)}, f32[9,48]{1,0:T(8,128)S(1)}) all-reduce(f32[2,64,48]{1,2,0:T(8,128)S(1)} %pad_maximum_fusion.8, f32[9,48]{1,0:T(8,128)S(1)} %convolution_bitcast_fusion.6), channel_id=1, replica_groups=mesh['ens'=2,'lat'=32,'chan'=8] {'ens','lat'}, use_global_device_ids=true, to_apply=%region_5.6 | all-reduce | flops 6576 | bytes 52608 | tf_op jit(solution)/shard_map/psum | solution.py:323
  468.7 6.5 %fusion.4 = bf16[1,48,4,256]{3,1,2,0:T(8,128)(2,1)S(1)} fusion(bf16[48,4,128]{0,2,1:T(8,128)(2,1)S(1)} %bitcast.622, bf16[48,4,256]{2,0,1:T(8,128)(2,1)S(1)} %all_to_all.100, bf16[48,8,256]{2,0,1:T(8,128)(2,1)S(1)} %get-tuple-element.539, bf16[48,8,8]{2,0,1:T(8,128)(2,1)S(1)} %get-tuple-element.520, bf16[48,8,8]{2,0,1:T(8,128)(2,1)S(1)} %get-tuple-element.519, ...), kind=kOutput, calls=%fused_computation.177 | convolution fusion | flops 37191680 | bytes 1076992 | tf_op jit(solution)/shard_map/dot_general | solution.py:275
  475.9 1.5 dynamic-slice_multiply_fusion
  477.5 1.4 dynamic-slice_multiply_fusion.1
  (449 shorter events, 37.7 us)
Async XLA Ops:
  9.7 77.4 %all-to-all-start = ((bf16[32,2,384]{2,1,0:T(2,128)(2,1)}), bf16[32,2,384]{2,1,0:T(2,128)(2,1)S(1)}, u32[]{:S(2)}, u32[]{:S(2)}) async-start(bf16[32,2,384]{2,1,0:T(2,128)(2,1)} %reshape.55196), calls=%async_computation | async-start | bytes 98304 | tf_op jit(solution)/shard_map/all_to_all | solution.py:157
  19.6 67.3 %collective-permute-start = (bf16[48,2,256]{2,0,1:T(8,128)(2,1)S(1)}, bf16[48,2,256]{2,0,1:T(8,128)(2,1)S(1)}, u32[]{:S(2)}, u32[]{:S(2)}) collective-permute-start(bf16[48,2,256]{2,0,1:T(8,128)(2,1)S(1)} %get-tuple-element.537), channel_id=1, source_target_pairs={{0,8},{8,16},{16,24},{24,32},{32,40},{40,48},{48,56},{56,64},{64,7... | collective-permute-start | bytes 147464 | tf_op jit(solution)/shard_map/ppermute | solution.py:23
  23.0 63.9 %collective-permute-start.1 = (bf16[48,2,256]{2,0,1:T(8,128)(2,1)S(1)}, bf16[48,2,256]{2,0,1:T(8,128)(2,1)S(1)}, u32[]{:S(2)}, u32[]{:S(2)}) collective-permute-start(bf16[48,2,256]{2,0,1:T(8,128)(2,1)S(1)} %get-tuple-element.536), channel_id=1, source_target_pairs={{8,0},{16,8},{24,16},{32,24},{40,32},{48,40},{56,48},{64,56},{72,6... | collective-permute-start | bytes 147464 | tf_op jit(solution)/shard_map/ppermute | solution.py:26
  89.2 12.5 %all-to-all-start.1 = ((bf16[32,2,384]{2,1,0:T(2,128)(2,1)}), bf16[32,2,384]{2,1,0:T(2,128)(2,1)S(1)}, u32[]{:S(2)}, u32[]{:S(2)}) async-start(bf16[32,2,384]{2,1,0:T(2,128)(2,1)} %reshape.55198), calls=%async_computation.1 | async-start | bytes 98304 | tf_op jit(solution)/shard_map/all_to_all | solution.py:161
  101.7 15.8 %all-to-all-start.3 = ((bf16[8,2,3072]{2,1,0:T(2,128)(2,1)}), bf16[8,2,3072]{2,1,0:T(2,128)(2,1)S(1)}, u32[]{:S(2)}, u32[]{:S(2)}) async-start(bf16[8,2,3072]{2,1,0:T(2,128)(2,1)} %reshape.55202), calls=%async_computation.3 | async-start | bytes 196608 | tf_op jit(solution)/shard_map/all_to_all | solution.py:207
  117.6 15.1 %all-to-all-start.2 = ((bf16[8,2,3072]{2,1,0:T(2,128)(2,1)}), bf16[8,2,3072]{2,1,0:T(2,128)(2,1)S(1)}, u32[]{:S(2)}, u32[]{:S(2)}) async-start(bf16[8,2,3072]{2,1,0:T(2,128)(2,1)} %reshape.55200), calls=%async_computation.2 | async-start | bytes 196608 | tf_op jit(solution)/shard_map/all_to_all | solution.py:243
  138.8 12.0 %all-to-all-start.4 = ((bf16[8,2,3072]{2,1,0:T(2,128)(2,1)}), bf16[8,2,3072]{2,1,0:T(2,128)(2,1)S(1)}, u32[]{:S(2)}, u32[]{:S(2)}) async-start(bf16[8,2,3072]{2,1,0:T(2,128)(2,1)} %reshape.55204), calls=%async_computation.4 | async-start | bytes 196608 | tf_op jit(solution)/shard_map/all_to_all | solution.py:252
  142.2 333.7 %all-reduce.7.cloned.1.call-start = ((), (), s32[]{:S(2)}) async-start(), calls=%async_computation.7 | async-start | bytes 4718592 | tf_op jit(solution)/shard_map/psum | solution.py:324
  158.3 19.9 %all-to-all-start.5 = ((bf16[32,2,384]{2,1,0:T(2,128)(2,1)}), bf16[32,2,384]{2,1,0:T(2,128)(2,1)S(1)}, u32[]{:S(2)}, u32[]{:S(2)}) async-start(bf16[32,2,384]{2,1,0:T(2,128)(2,1)} %reshape.55206), calls=%async_computation.5 | async-start | bytes 98304 | tf_op jit(solution)/shard_map/all_to_all | solution.py:157
  166.9 11.1 %collective-permute-start.2 = (bf16[48,2,256]{2,0,1:T(8,128)(2,1)S(1)}, bf16[48,2,256]{2,0,1:T(8,128)(2,1)S(1)}, u32[]{:S(2)}, u32[]{:S(2)}) collective-permute-start(bf16[48,2,256]{2,0,1:T(8,128)(2,1)S(1)} %get-tuple-element.535), channel_id=1, source_target_pairs={{0,8},{8,16},{16,24},{24,32},{32,40},{40,48},{48,56},{56,64},{64,7... | collective-permute-start | bytes 147464 | tf_op jit(solution)/shard_map/ppermute | solution.py:23
  170.3 7.8 %collective-permute-start.3 = (bf16[48,2,256]{2,0,1:T(8,128)(2,1)S(1)}, bf16[48,2,256]{2,0,1:T(8,128)(2,1)S(1)}, u32[]{:S(2)}, u32[]{:S(2)}) collective-permute-start(bf16[48,2,256]{2,0,1:T(8,128)(2,1)S(1)} %get-tuple-element.534), channel_id=1, source_target_pairs={{8,0},{16,8},{24,16},{32,24},{40,32},{48,40},{56,48},{64,56},{72,6... | collective-permute-start | bytes 147464 | tf_op jit(solution)/shard_map/ppermute | solution.py:26
  178.8 289.6 %copy-start.7 = (f32[48,4,1,1]{0,3,2,1:T(1,128)S(1)}, f32[48,4,1,1]{0,3,2,1:T(1,128)}, u32[]{:S(2)}) copy-start(f32[48,4,1,1]{0,3,2,1:T(1,128)} %get-tuple-element.400) | copy-start | bytes 2308
  178.8 289.6 %copy-start.8 = (f32[48,4,1,1]{0,3,2,1:T(1,128)S(1)}, f32[48,4,1,1]{0,3,2,1:T(1,128)}, u32[]{:S(2)}) copy-start(f32[48,4,1,1]{0,3,2,1:T(1,128)} %get-tuple-element.401) | copy-start | bytes 2308
  178.8 289.6 %copy-start.9 = (f32[48,4,1,1]{0,3,2,1:T(1,128)S(1)}, f32[48,4,1,1]{0,3,2,1:T(1,128)}, u32[]{:S(2)}) copy-start(f32[48,4,1,1]{0,3,2,1:T(1,128)} %get-tuple-element.402) | copy-start | bytes 2308
  178.8 289.6 %copy-start.10 = (f32[48,4,1,1]{0,3,2,1:T(1,128)S(1)}, f32[48,4,1,1]{0,3,2,1:T(1,128)}, u32[]{:S(2)}) copy-start(f32[48,4,1,1]{0,3,2,1:T(1,128)} %get-tuple-element.403) | copy-start | bytes 2308
  178.8 289.6 %copy-start.11 = (f32[48,4,1,1]{0,3,2,1:T(1,128)S(1)}, f32[48,4,1,1]{0,3,2,1:T(1,128)}, u32[]{:S(2)}) copy-start(f32[48,4,1,1]{0,3,2,1:T(1,128)} %get-tuple-element.404) | copy-start | bytes 2308
  178.8 289.6 %copy-start.12 = (f32[48,4,1,1]{0,3,2,1:T(1,128)S(1)}, f32[48,4,1,1]{0,3,2,1:T(1,128)}, u32[]{:S(2)}) copy-start(f32[48,4,1,1]{0,3,2,1:T(1,128)} %get-tuple-element.405) | copy-start | bytes 2308
  178.8 289.6 %copy-start.13 = (f32[48,4,1,1]{0,3,2,1:T(1,128)S(1)}, f32[48,4,1,1]{0,3,2,1:T(1,128)}, u32[]{:S(2)}) copy-start(f32[48,4,1,1]{0,3,2,1:T(1,128)} %get-tuple-element.406) | copy-start | bytes 2308
  178.8 289.6 %copy-start.14 = (f32[48,4,1,1]{0,3,2,1:T(1,128)S(1)}, f32[48,4,1,1]{0,3,2,1:T(1,128)}, u32[]{:S(2)}) copy-start(f32[48,4,1,1]{0,3,2,1:T(1,128)} %get-tuple-element.407) | copy-start | bytes 2308
  178.9 289.6 %copy-start.15 = (f32[48,4,1,1]{0,3,2,1:T(1,128)S(1)}, f32[48,4,1,1]{0,3,2,1:T(1,128)}, u32[]{:S(2)}) copy-start(f32[48,4,1,1]{0,3,2,1:T(1,128)} %get-tuple-element.408) | copy-start | bytes 2308
  178.9 289.6 %copy-start.16 = (f32[48,4,1,1]{0,3,2,1:T(1,128)S(1)}, f32[48,4,1,1]{0,3,2,1:T(1,128)}, u32[]{:S(2)}) copy-start(f32[48,4,1,1]{0,3,2,1:T(1,128)} %get-tuple-element.409) | copy-start | bytes 2308
  178.9 289.6 %copy-start.17 = (f32[48,4,1,1]{0,3,2,1:T(1,128)S(1)}, f32[48,4,1,1]{0,3,2,1:T(1,128)}, u32[]{:S(2)}) copy-start(f32[48,4,1,1]{0,3,2,1:T(1,128)} %get-tuple-element.410) | copy-start | bytes 2308
  178.9 289.6 %copy-start.18 = (f32[48,4,1,1]{0,3,2,1:T(1,128)S(1)}, f32[48,4,1,1]{0,3,2,1:T(1,128)}, u32[]{:S(2)}) copy-start(f32[48,4,1,1]{0,3,2,1:T(1,128)} %get-tuple-element.411) | copy-start | bytes 2308
  180.3 287.7 %all-to-all-start.6 = ((bf16[32,2,384]{2,1,0:T(2,128)(2,1)}), bf16[32,2,384]{2,1,0:T(2,128)(2,1)S(1)}, u32[]{:S(2)}, u32[]{:S(2)}) async-start(bf16[32,2,384]{2,1,0:T(2,128)(2,1)} %reshape.55208), calls=%async_computation.6 | async-start | bytes 98304 | tf_op jit(solution)/shard_map/all_to_all | solution.py:161
  (71 other events, 7585.3 us)
Sparse Core Ops, SparseCore 0:
  148.1 279.6 all-reduce.6
where the time goes:
time: 487 us; the launch traced here: 486 us
  blocking collectives  277 us (57%)
  starting transfers between devices  71.5 us (15%)
  between operations  58.2 us (12%)
  local copies, waits for them, and re-layouts  24.1 us (5%)
  matrix products  20.6 us (4%)
  waiting for transfers between devices  20.2 us (4%)
  other arithmetic  14.3 us (3%)
    psum x1, blocking collectives, shards(): lax.psum((filter_part, disco_part), ('ens', 'lat'))  277 us
    all_to_all x2, starting transfers between devices, to_modes(): lax.all_to_all(spectrum, 'lat', split_axis=3, concat_axis=1, tiled=True)  18.5 us
    all_to_all x2, starting transfers between devices, to_bands(): lax.all_to_all(spectrum, 'lat', split_axis=1, concat_axis=3, tiled=True)  17.6 us
    ppermute x2, starting transfers between devices, padded_2(): lax.ppermute(lax.slice_in_dim(block, 0, width, axis=dim), axis, backward)  11.6 us
  transfers between devices with their start and end apart: 12, of which 4 were waited for; matrix products, arithmetic and copies ran while one was open for 9% of the time, Pallas kernels for 0%

commit v1 on v0

v1 whole, which is shorter than its diff:
```python
import functools
import math

import jax
import jax.numpy as jnp
import ml_dtypes
import numpy as np
from jax import lax
from jax.experimental import pallas as pl
from jax.experimental.pallas import tpu as pltpu
from jax.sharding import PartitionSpec as P

MESH = pl.DeviceIdType.MESH
HALO = 2
LANES = 128
norm_eps = 1e-06
inv_root_two = 0.7071067811865476
inv_root_tau = 0.3989422804014327
f32 = jnp.float32
bf16 = jnp.bfloat16
NT = (((1,), (1,)), ((), ()))


def legendre_table(lat_count, order_count, degree_count):
    theta = math.pi * (np.arange(lat_count) + 0.5) / lat_count
    cosine, sine = np.cos(theta), np.sin(theta)
    table = np.zeros((order_count, degree_count, lat_count))
    for m in range(order_count):
        start = 0.5 * (
            math.log((2 * m + 1) / (4 * math.pi))
            + math.lgamma(m + 0.5)
            - math.lgamma(m + 1)
            - math.lgamma(0.5)
        )
        if m < degree_count:
            table[m, m] = np.exp(start + m * np.log(sine))
        for l in range(m + 1, degree_count):
            a = math.sqrt((4 * l * l - 1) / (l * l - m * m))
            b = math.sqrt(((l - 1) ** 2 - m * m) / (4 * (l - 1) ** 2 - 1))
            before = table[m, l - 2] if l >= 2 else 0.0
            table[m, l] = a * (cosine * table[m, l - 1] - b * before)
    return table


def constant_tables(lat_count, lon_count, mode_count, degree_count, bands):
    legendre = legendre_table(lat_count, mode_count, degree_count)
    sine = np.sin(math.pi * (np.arange(lat_count) + 0.5) / lat_count)
    quadrature = (2 * math.pi / lon_count) * (math.pi / lat_count) * sine
    here = mode_count // bands
    shape = (bands, here * degree_count, lat_count)
    plain = legendre.reshape(shape).astype(np.float32).astype(ml_dtypes.bfloat16)
    weighted = (legendre * quadrature).reshape(shape).astype(np.float32).astype(ml_dtypes.bfloat16)
    modes = np.arange(mode_count)
    phase = 2 * math.pi * ((modes[:, None] * np.arange(lon_count)[None, :]) % lon_count) / lon_count
    scale = np.where(modes == 0, 1.0, 2.0)[:, None]
    cos_rows = np.cos(phase).reshape(bands, 1, here, lon_count)
    sin_rows = -np.sin(phase).reshape(bands, 1, here, lon_count)
    forward = np.concatenate([cos_rows, sin_rows], axis=1).reshape(2 * mode_count, lon_count)
    doubled = np.repeat(scale.reshape(bands, 1, here, 1), 2, axis=1).reshape(2 * mode_count, 1)
    cast = lambda v: v.astype(np.float32).astype(ml_dtypes.bfloat16)
    return plain, weighted, cast(forward), cast(forward * doubled)


class Names:
    def __init__(self, names, refs):
        for name, ref in zip(names, refs, strict=True):
            setattr(self, name, ref)


ARGS = (
    "field", "cot", "sw", "dw", "wh", "wo", "fwd", "inv", "coef", "rows", "shift", "p_hbm",
    "q_hbm", "gfield", "gsw", "gdw", "gh", "go",
)
DMAS = (
    "a1", "a2", "cot", "mix", "grd", "a5", "a6", "lo", "hi", "glo", "ghi", "re", "fa", "fb", "fc",
    "ra0", "ra1", "ra2", "rb0", "rb1", "rb2", "rc0", "rc1", "rc2", "rd0", "rd1", "rd2",
)
S = {name: i for i, name in enumerate(DMAS)}


def scratch(n):
    piece = n.qn * n.rows
    return dict(
        pt=pltpu.VMEM((n.ml * n.deg, n.lat), bf16),
        qt=pltpu.VMEM((n.ml * n.deg, n.lat), bf16),
        qa=pltpu.VMEM((n.qn * n.deg, n.nb * piece), bf16),
        pa=pltpu.VMEM((n.qn * n.deg, n.nb * piece), bf16),
        qb=pltpu.VMEM((n.nb * piece, n.qn * n.deg), bf16),
        pb=pltpu.VMEM((n.nb * piece, n.qn * n.deg), bf16),
        wht=pltpu.VMEM((n.hid, n.chans), bf16),
        spread_rows=pltpu.VMEM((n.nb * piece, LANES), f32),
        s1=pltpu.VMEM((n.nb, piece, LANES), bf16),
        r1=pltpu.VMEM((n.nb, piece, LANES), bf16),
        s2=pltpu.VMEM((n.nb, piece, LANES), bf16),
        r2=pltpu.VMEM((n.nb, piece, LANES), bf16),
        s5=pltpu.VMEM((n.nb, piece, LANES), bf16),
        r5=pltpu.VMEM((n.nb, piece, LANES), bf16),
        s6=pltpu.VMEM((n.nb, piece, LANES), bf16),
        r6=pltpu.VMEM((n.nb, piece, LANES), bf16),
        coeffs=pltpu.VMEM((n.qn * n.deg, LANES), f32),
        sww=pltpu.VMEM((2, n.ml * n.deg, LANES), f32),
        halo=pltpu.VMEM((2, HALO, n.cl, n.lon), bf16),
        ghalo=pltpu.VMEM((2, HALO, n.cl, n.lon), bf16),
        fext=pltpu.VMEM((n.rows + 2 * HALO, n.cl, n.lon), f32),
        gm=pltpu.VMEM((n.rows, n.cl, n.lon), bf16),
        shifted=pltpu.VMEM((n.rows * n.ks, n.cl, n.lon), f32),
        square=pltpu.VMEM((LANES, LANES), f32),
        wcol=pltpu.VMEM((n.ks, n.cl, n.lon), f32),
        disco=pltpu.VMEM((n.rows, n.cl, n.lon), f32),
        back=pltpu.VMEM((n.rows, n.cl, n.lon), f32),
        dgrad=pltpu.VMEM((LANES, LANES), f32),
        cotall=pltpu.VMEM((n.ng, n.cl, LANES), bf16),
        mixs=pltpu.VMEM((n.ng, n.cl, LANES), bf16),
        mixall=pltpu.VMEM((n.ng, n.cl, LANES), bf16),
        gact=pltpu.VMEM((n.hid, LANES), f32),
        gpre=pltpu.VMEM((n.hid, LANES), bf16),
        gs=pltpu.VMEM((n.ng, n.cl, LANES), bf16),
        gr=pltpu.VMEM((n.ng, n.cl, LANES), bf16),
        wide=pltpu.VMEM((n.cl, n.rows, n.lon), f32),
        fld=pltpu.VMEM((n.rows, n.cl, n.lon), bf16),
        cot8=pltpu.VMEM((n.ng, n.cl, LANES), bf16),
        n32=pltpu.VMEM((n.chans, LANES), f32),
        np32=pltpu.VMEM((n.chans, LANES), f32),
        ap32=pltpu.VMEM((n.hid, LANES), f32),
        was=pltpu.VMEM((2, n.kc, n.nx, n.hid // n.nx, LANES), bf16),
        war=pltpu.VMEM((n.kc, n.nx, n.hid // n.nx, LANES), bf16),
        wbs=pltpu.VMEM((n.kc, n.nx, n.hid // n.nx, LANES), bf16),
        wbr=pltpu.VMEM((n.kc, n.nx, n.hid // n.nx, LANES), bf16),
        wsum=pltpu.VMEM((n.hid // n.nx, LANES), f32),
        wslot=pltpu.VMEM((n.nz, n.slot, LANES), f32),
        wcs=pltpu.VMEM((n.kc, n.nz, n.slot, LANES), bf16),
        wcr=pltpu.VMEM((n.kc, n.nz, n.slot, LANES), bf16),
        wds=pltpu.VMEM((n.kc, n.slot, LANES), bf16),
        wdr=pltpu.VMEM((n.kc, n.ng, n.slot, LANES), bf16),
        wtot=pltpu.VMEM((2, n.kc, n.slot, LANES), f32),
        fas=pltpu.VMEM((n.nx, 2 * n.frows, LANES), bf16),
        far=pltpu.VMEM((n.nx, 2 * n.frows, LANES), bf16),
        fbs=pltpu.VMEM((2 * n.frows, LANES), bf16),
        fbr=pltpu.VMEM((2 * n.nz, 2 * n.frows, LANES), bf16),
        fcr=pltpu.VMEM((n.nx, n.frows, LANES), f32),
        load_sem=pltpu.SemaphoreType.DMA((2,)),
        send=pltpu.SemaphoreType.DMA((len(DMAS),)),
        recv=pltpu.SemaphoreType.DMA((len(DMAS),)),
    )


def kernel(n, names, *refs):
    v = Names(list(names), refs)
    me_e, me_b, me_g = (lax.axis_index(a) for a in ("ens", "lat", "chan"))
    me_z, me_x = lax.div(me_b, n.nx), lax.rem(me_b, n.nx)
    first = me_b * n.rows
    piece = n.qn * n.rows
    total_rows = n.nb * piece

    def copy(phase, src, dst, device):
        return pltpu.make_async_remote_copy(
            src_ref=src,
            dst_ref=dst,
            send_sem=v.send.at[S[phase]],
            recv_sem=v.recv.at[S[phase]],
            device_id=device,
            device_id_type=MESH,
        )

    def arrived(phase, ref):
        pltpu.make_async_copy(ref, ref, v.recv.at[S[phase]]).wait()

    def left(phase, ref):
        pltpu.make_async_copy(ref, ref, v.send.at[S[phase]]).wait()

    def lat_peer(k):
        return lax.rem(me_b + k, n.nb)

    def lat_at(t):
        u = lax.div(t, n.nx)
        far = n.nz // 2
        dz = jnp.where(lax.rem(u, 2) == 0, far - lax.div(u, 2), far + lax.div(u + 1, 2))
        dx = lax.rem(n.nx // 2 + n.nx - lax.rem(t, n.nx), n.nx)
        dx = jnp.where(u == n.nz - 1, n.nx // 2 + lax.rem(t, n.nx) - 1, dx)
        return lax.rem(me_z + n.nz + dz, n.nz) * n.nx + lax.rem(me_x + n.nx + dx, n.nx)

    def exchange(phase, axis, me, count, src, dst, whole=False):
        def step(k, carry):
            d = lax.rem(me + k, count)
            copy(phase, src if whole else src.at[d], dst.at[me], {axis: d}).start()
            return carry

        def to_lat(t, carry):
            d = lat_at(t)
            copy(phase, src.at[d], dst.at[me], {axis: d}).start()
            return carry

        if axis == "lat":
            lax.fori_loop(0, count - 1, to_lat, 0)
        else:
            lax.fori_loop(1, count, step, 0)
        dst[me] = src[...] if whole else src[me]

    barrier = pltpu.get_barrier_semaphore()

    def greet(device):
        pl.semaphore_signal(barrier, inc=1, device_id=device, device_id_type=MESH)

    def greet_lat(k, carry):
        greet({"lat": lat_at(k)})
        return carry

    def greet_chan(k, carry):
        greet({"chan": lax.rem(me_g + k, n.ng)})
        return carry

    def greet_ens(k, carry):
        greet({"ens": 1 - me_e, "lat": k * n.nx + me_x})
        return carry

    lax.fori_loop(0, n.nb - 1, greet_lat, 0)
    lax.fori_loop(1, n.ng, greet_chan, 0)
    lax.fori_loop(0, n.nz, greet_ens, 0)

    load_p = pltpu.make_async_copy(v.p_hbm.at[me_b], v.pt, v.load_sem.at[0])
    load_q = pltpu.make_async_copy(v.q_hbm.at[me_b], v.qt, v.load_sem.at[1])
    load_p.start()
    load_q.start()

    def to_pieces(table, row_of, out):
        for r in range(n.rows):
            part = lax.dot_general(table[...], row_of(r), NT, preferred_element_type=f32)
            v.spread_rows[pl.ds(r, 2 * n.modes, stride=n.rows), :] = jnp.concatenate(
                [part, jnp.zeros((2 * n.modes, LANES - n.cl), f32)], axis=1
            )
        out[...] = v.spread_rows[...].astype(bf16).reshape(n.nb, piece, LANES)

    def from_pieces(table, pieces):
        v.spread_rows[...] = pieces[...].reshape(total_rows, LANES).astype(f32)
        rows = []
        for r in range(n.rows):
            part = v.spread_rows[pl.ds(r, 2 * n.modes, stride=n.rows), :]
            flipped = jnp.transpose(part).astype(bf16)[: n.cl]
            rows.append(jnp.dot(flipped, table[...], preferred_element_type=f32))
        return rows

    v.wide[...] = v.field[...].astype(f32)
    for r in range(n.rows):
        row = v.wide[:, r, :]
        v.fext[HALO + r] = row
        v.fld[r] = row.astype(bf16)
    to_pieces(v.fwd, lambda r: v.fld[r], v.s1)
    v.wide[...] = v.cot[...].astype(f32)
    for r in range(n.rows):
        row = v.wide[:, r, :].astype(bf16)
        v.cot8[2 * r] = row[:, :LANES]
        v.cot8[2 * r + 1] = row[:, LANES:]
    pl.semaphore_wait(barrier, n.nb - 1 + n.ng - 1 + n.nz)

    exchange("a1", "lat", me_b, n.nb, v.s1, v.r1)
    below, above = lat_peer(n.nb - 1), lat_peer(1)
    top, bottom = pl.ds(0, HALO), pl.ds(n.rows - HALO, HALO)
    copy("hi", v.fld.at[top], v.halo.at[1], {"lat": below}).start()
    copy("lo", v.fld.at[bottom], v.halo.at[0], {"lat": above}).start()
    exchange("cot", "chan", me_g, n.ng, v.cot8, v.cotall)

    load_p.wait()
    load_q.wait()

    half = n.ml * n.deg
    wide = (n.lat, total_rows)
    column = lax.broadcasted_iota(jnp.int32, wide, 1)
    row_id = lax.broadcasted_iota(jnp.int32, wide, 0)
    lat_of = lax.div(column, piece) * n.rows + lax.rem(column, n.rows)
    expand = jnp.where(lat_of == row_id, 1.0, 0.0).astype(bf16)
    q_of = lax.div(lax.rem(lax.broadcasted_iota(jnp.int32, (half, total_rows), 1), piece), n.rows)
    ml_of = lax.div(lax.broadcasted_iota(jnp.int32, (half, total_rows), 0), n.deg)

    def expanded(table, out):
        both = jnp.dot(table[...], expand, preferred_element_type=f32)
        for t in range(2):
            keep = q_of == ml_of + t * n.ml
            out[t * half : (t + 1) * half, :] = jnp.where(keep, both, 0.0).astype(bf16)

    expanded(v.qt, v.qa)
    expanded(v.pt, v.pa)
    for t in range(2):
        mine = slice(t * half, (t + 1) * half)
        v.pb[:, mine] = jnp.transpose(v.pa[mine, :].astype(f32)).astype(bf16)
    v.square[...] = jnp.zeros((LANES, LANES), f32)
    for t in range(2):
        v.square[: n.cl, : n.deg] = v.sw[t]
        block = jnp.transpose(v.square[...])[: n.deg]
        for m in range(n.ml):
            v.sww[t, m * n.deg : (m + 1) * n.deg, :] = block

    arrived("a1", v.r1.at[pl.ds(0, n.nb - 1)])
    spectrum = v.r1[...].reshape(total_rows, LANES)
    coeffs = jnp.dot(v.qa[...], spectrum, preferred_element_type=f32)
    v.coeffs[...] = coeffs
    real, imag = coeffs[:half], coeffs[half:]
    s0, s1 = v.sww[0], v.sww[1]
    filtered = jnp.concatenate([s0 * real - s1 * imag, s0 * imag + s1 * real], axis=0)
    synth = jnp.dot(v.pb[...], filtered.astype(bf16), preferred_element_type=f32)
    v.s2[...] = synth.astype(bf16).reshape(n.nb, piece, LANES)
    exchange("a2", "lat", me_b, n.nb, v.s2, v.r2)

    v.square[...] = jnp.zeros((LANES, LANES), f32)
    v.square[: n.ks, : n.cl] = v.dw[...]
    columns = jnp.transpose(v.square[...])
    for k in range(n.ks):
        v.wcol[k] = jnp.broadcast_to(columns[: n.cl, k : k + 1], (n.cl, n.lon))
    arrived("lo", v.halo.at[0])
    arrived("hi", v.halo.at[1])
    for r in range(HALO):
        v.fext[r] = v.halo[0, r].astype(f32)
        v.fext[HALO + n.rows + r] = v.halo[1, r].astype(f32)

    for r in range(n.rows):

        def tap(k, total, r=r):
            source = v.rows[k, first + r] - first + HALO
            source = jnp.minimum(jnp.maximum(source, 0), n.rows + 2 * HALO - 1)
            amount = lax.rem(n.lon - v.shift[k, first + r], n.lon)
            moved = pltpu.roll(v.fext[source], amount, 1)
            v.shifted[r * n.ks + k] = moved
            return total + (v.coef[k, first + r] * v.wcol[k]) * moved

        v.disco[r] = lax.fori_loop(0, n.ks, tap, jnp.zeros((n.cl, n.lon), f32))

    for t in range(2):
        mine = slice(t * half, (t + 1) * half)
        v.qb[:, mine] = jnp.transpose(v.qa[mine, :].astype(f32)).astype(bf16)
    v.wht[...] = jnp.transpose(v.wh[...].astype(f32)).astype(bf16)
    arrived("cot", v.cotall.at[pl.ds(0, n.ng - 1)])
    v.gact[...] = jnp.dot(
        v.wo[...], v.cotall[...].reshape(n.chans, LANES), preferred_element_type=f32
    )

    arrived("a2", v.r2.at[pl.ds(0, n.nb - 1)])
    for r, row in enumerate(from_pieces(v.inv, v.r2)):
        mixed = (row + v.disco[r]).astype(bf16)
        v.mixs[2 * r] = mixed[:, :LANES]
        v.mixs[2 * r + 1] = mixed[:, LANES:]
    exchange("mix", "chan", me_g, n.ng, v.mixs, v.mixall)

    arrived("mix", v.mixall.at[pl.ds(0, n.ng - 1)])
    mixed = v.mixall[...].reshape(n.chans, LANES).astype(f32)
    rscale = lax.rsqrt(jnp.sum(mixed * mixed, axis=0, keepdims=True) * (1.0 / n.chans) + norm_eps)
    normed32 = mixed * rscale
    normed = normed32.astype(bf16)
    v.n32[...] = normed32
    preact = jnp.dot(v.wht[...], normed, preferred_element_type=f32)
    cumulative = 0.5 * (1.0 + lax.erf(preact * inv_root_two))
    density = jnp.exp(-0.5 * preact * preact) * inv_root_tau
    activated = preact * cumulative
    grad_pre = (v.gact[...] * (cumulative + preact * density)).astype(bf16)
    v.gpre[...] = grad_pre
    grad_normed = jnp.dot(v.wh[...], grad_pre, preferred_element_type=f32)
    along = jnp.sum(grad_normed * normed32, axis=0, keepdims=True) * (1.0 / n.chans)
    grad_mixed = (rscale * (grad_normed - normed32 * along)).astype(bf16)
    v.gs[...] = grad_mixed.reshape(n.ng, n.cl, LANES)
    exchange("grd", "chan", me_g, n.ng, v.gs, v.gr)

    share = n.chans // n.nb
    for x in range(n.nx):
        for z in range(n.nz):
            at, to = (z * n.nx + x) * share, (x * n.nz + z) * share
            v.np32[to : to + share, :] = v.n32[at : at + share, :]
            v.ap32[2 * to : 2 * (to + share), :] = activated[2 * at : 2 * (at + share)]
    normed = v.np32[...].astype(bf16)
    activated = v.ap32[...].astype(bf16)
    adjoint = v.cotall[...].reshape(n.chans, LANES)
    cols, depth = n.chans // n.nx, n.hid // n.nx

    def r_a(k):
        for half in range(2):
            at = half * n.chans + k * LANES
            hidden = lax.dot_general(
                normed, v.gpre[at : at + LANES, :], NT, preferred_element_type=f32
            ).astype(bf16)
            for x in range(n.nx):
                rows = hidden[x * cols : (x + 1) * cols]
                v.was[0, k, x, half * cols : (half + 1) * cols, :] = rows
        output = lax.dot_general(
            activated, adjoint[k * LANES : (k + 1) * LANES], NT, preferred_element_type=f32
        )
        v.was[1, k] = output.astype(bf16).reshape(n.nx, depth, LANES)
        copy(f"ra{k}", v.was.at[1 - me_e, k], v.war.at[k], {"ens": 1 - me_e}).start()

    def r_b(k):
        arrived(f"ra{k}", v.war.at[k])
        v.wbs[k] = (v.was[me_e, k].astype(f32) + v.war[k].astype(f32)).astype(bf16)

        def send(t, carry):
            x = lax.rem(me_x + t, n.nx)
            copy(f"rb{k}", v.wbs.at[k, x], v.wbr.at[k, me_x], {"lat": me_z * n.nx + x}).start()
            return carry

        lax.fori_loop(1, n.nx, send, 0)
        v.wbr[k, me_x] = v.wbs[k, me_x]

    def r_c(k):
        arrived(f"rb{k}", v.wbr.at[k, pl.ds(0, n.nx - 1)])
        v.wsum[...] = jnp.sum(v.wbr[k].astype(f32), axis=0)

        @pl.when(me_e == 0)
        def _():
            for z in range(n.nz):
                for half in range(2):
                    at, to = half * cols + z * share, half * (n.slot // 2)
                    v.wslot[z, to : to + share, :] = v.wsum[at : at + share, :]

        @pl.when(me_e == 1)
        def _():
            for z in range(n.nz):
                v.wslot[z, : 2 * share, :] = v.wsum[2 * z * share : 2 * (z + 1) * share, :]

        v.wcs[k] = v.wslot[...].astype(bf16)

        def send(t, carry):
            z = lax.rem(me_z + t, n.nz)
            copy(f"rc{k}", v.wcs.at[k, z], v.wcr.at[k, me_z], {"lat": z * n.nx + me_x}).start()
            return carry

        lax.fori_loop(1, n.nz, send, 0)
        v.wcr[k, me_z] = v.wcs[k, me_z]

    def r_d(k):
        arrived(f"rc{k}", v.wcr.at[k, pl.ds(0, n.nz - 1)])
        v.wds[k] = jnp.sum(v.wcr[k].astype(f32), axis=0).astype(bf16)

        def send(t, carry):
            g = lax.rem(me_g + t, n.ng)
            copy(f"rd{k}", v.wds.at[k], v.wdr.at[k, me_g], {"chan": g}).start()
            return carry

        lax.fori_loop(1, n.ng, send, 0)
        v.wdr[k, me_g] = v.wds[k]

    def r_e(k):
        arrived(f"rd{k}", v.wdr.at[k, pl.ds(0, n.ng - 1)])
        v.wtot[me_e, k] = jnp.sum(v.wdr[k].astype(f32), axis=0)

    for k in range(n.kc):
        r_a(k)
    for k in range(n.kc):
        r_b(k)

    arrived("grd", v.gr.at[pl.ds(0, n.ng - 1)])
    for r in range(n.rows):
        v.gm[r] = jnp.concatenate([v.gr[2 * r], v.gr[2 * r + 1]], axis=1)
    to_pieces(v.inv, lambda r: v.gm[r], v.s5)
    exchange("a5", "lat", me_b, n.nb, v.s5, v.r5)
    copy("ghi", v.gm.at[top], v.ghalo.at[1], {"lat": below}).start()
    copy("glo", v.gm.at[bottom], v.ghalo.at[0], {"lat": above}).start()

    lane = lax.broadcasted_iota(jnp.int32, (n.cl, LANES), 1)

    def weight_tap(k, total):
        inner = jnp.zeros((n.cl, n.lon), f32)
        for r in range(n.rows):
            inner = inner + v.coef[k, first + r] * (
                v.shifted[r * n.ks + k] * v.gm[r].astype(f32)
            )
        return total + jnp.where(lane == k, jnp.sum(inner, axis=1, keepdims=True), 0.0)

    weight_grad = lax.fori_loop(0, n.ks, weight_tap, jnp.zeros((n.cl, LANES), f32))
    v.square[...] = jnp.zeros((LANES, LANES), f32)
    v.square[: n.cl, :] = weight_grad
    v.dgrad[...] = jnp.transpose(v.square[...])

    for r in range(n.rows):
        v.back[r] = jnp.zeros((n.cl, n.lon), f32)

    def spread(at, rows_of):
        values = rows_of.astype(f32)
        wanted = first - HALO + at
        held = jnp.minimum(jnp.maximum(wanted, 0), n.lat - 1)
        real_row = jnp.where(held == wanted, 1.0, 0.0).astype(f32)
        targets = [r for r in range(n.rows) if abs(at - HALO - r) <= HALO]

        def tap(k, totals):
            moved = pltpu.roll(values, lax.rem(n.lon + v.shift[k, held], n.lon), 1) * v.wcol[k]
            factor = v.coef[k, held] * real_row
            to = v.rows[k, held]
            return tuple(
                total + jnp.where(to == first + r, factor, 0.0) * moved
                for r, total in zip(targets, totals)
            )

        start = tuple(v.back[r] for r in targets)
        for r, total in zip(targets, lax.fori_loop(0, n.ks, tap, start)):
            v.back[r] = total

    for r in range(n.rows):
        if r == n.rows // 2:
            r_c(0)
        spread(HALO + r, v.gm[r])
    r_c(1)

    arrived("a5", v.r5.at[pl.ds(0, n.nb - 1)])
    grads = jnp.dot(v.pa[...], v.r5[...].reshape(total_rows, LANES), preferred_element_type=f32)
    g_real, g_imag = grads[:half], grads[half:]
    s0, s1 = v.sww[0], v.sww[1]
    g_coeffs = jnp.concatenate([s0 * g_real + s1 * g_imag, s0 * g_imag - s1 * g_real], axis=0)
    back_spec = jnp.dot(v.qb[...], g_coeffs.astype(bf16), preferred_element_type=f32)
    v.s6[...] = back_spec.astype(bf16).reshape(n.nb, piece, LANES)
    exchange("a6", "lat", me_b, n.nb, v.s6, v.r6)

    real, imag = v.coeffs[:half, :], v.coeffs[half:, :]
    terms = (g_real * real + g_imag * imag, g_imag * real - g_real * imag)
    parts = []
    for t in range(2):
        part = terms[t][: n.deg]
        for m in range(1, n.ml):
            part = part + terms[t][m * n.deg : (m + 1) * n.deg]
        parts.append(part)
    low_lanes = lax.broadcasted_iota(jnp.int32, (n.deg, LANES), 1) < 64
    both = jnp.where(low_lanes, parts[0], pltpu.roll(parts[1], 64, 1))
    for x in range(n.nx):
        v.fas[x, : n.frows, :] = both[x * n.frows : (x + 1) * n.frows].astype(bf16)
        v.fas[x, n.frows :, :] = v.dgrad[: n.frows, :].astype(bf16)

    def send_fa(t, carry):
        x = lax.rem(me_x + t, n.nx)
        copy("fa", v.fas.at[x], v.far.at[me_x], {"lat": me_z * n.nx + x}).start()
        return carry

    lax.fori_loop(1, n.nx, send_fa, 0)
    v.far[me_x] = v.fas[me_x]
    r_c(2)

    arrived("glo", v.ghalo.at[0])
    arrived("ghi", v.ghalo.at[1])
    spread(0, v.ghalo[0, 0])
    spread(1, v.ghalo[0, 1])

    place = me_e * n.nz + me_z
    arrived("fa", v.far.at[pl.ds(0, n.nx - 1)])
    v.fbs[...] = jnp.sum(v.far[...].astype(f32), axis=0).astype(bf16)

    def send_fb(t, carry):
        p = lax.rem(place + t, 2 * n.nz)
        to = {"ens": lax.div(p, n.nz), "lat": lax.rem(p, n.nz) * n.nx + me_x}
        copy("fb", v.fbs, v.fbr.at[place], to).start()
        return carry

    lax.fori_loop(1, 2 * n.nz, send_fb, 0)
    v.fbr[place] = v.fbs[...]
    r_d(0)

    spread(HALO + n.rows, v.ghalo[1, 0])
    spread(HALO + n.rows + 1, v.ghalo[1, 1])
    r_d(1)
    r_d(2)

    arrived("a6", v.r6.at[pl.ds(0, n.nb - 1)])
    for r, row in enumerate(from_pieces(v.fwd, v.r6)):
        base = jnp.concatenate([v.cot8[2 * r], v.cot8[2 * r + 1]], axis=1).astype(f32)
        v.wide[:, r, :] = base + row + v.back[r]
    v.gfield[...] = v.wide[...].astype(bf16)

    arrived("fb", v.fbr.at[pl.ds(0, 2 * n.nz - 1)])
    ftot = jnp.sum(v.fbr[...].astype(f32), axis=0)
    v.fcr[me_x] = ftot[: n.frows]

    def send_fc(t, carry):
        x = lax.rem(me_x + t, n.nx)
        copy("fc", v.fcr.at[me_x], v.fcr.at[me_x], {"lat": me_z * n.nx + x}).start()
        return carry

    lax.fori_loop(1, n.nx, send_fc, 0)
    v.gdw[...] = ftot[n.frows : n.frows + n.ks, : n.cl] * n.scale

    for k in range(n.kc):
        r_e(k)
    copy("re", v.wtot.at[me_e], v.wtot.at[me_e], {"ens": 1 - me_e}).start()

    arrived("fc", v.fcr.at[pl.ds(0, n.nx - 1)])
    v.square[: n.deg, :] = v.fcr[...].reshape(n.deg, LANES)
    flipped = jnp.transpose(v.square[...])
    v.gsw[0] = flipped[: n.cl, : n.deg]
    v.gsw[1] = flipped[64 : 64 + n.cl, : n.deg]

    arrived("re", v.wtot.at[0])
    for k in range(n.kc):
        lanes = slice(k * LANES, (k + 1) * LANES)
        upper = slice(n.chans + k * LANES, n.chans + (k + 1) * LANES)
        low = n.slot // 2
        v.gh[:, lanes] = v.wtot[0, k, :share, :] * n.scale
        v.gh[:, upper] = v.wtot[0, k, low : low + share, :] * n.scale
        v.go[:, lanes] = v.wtot[1, k, : 2 * share, :] * n.scale

    for phase, ref in (("a1", v.s1), ("a2", v.s2), ("a5", v.s5), ("a6", v.s6)):
        left(phase, ref.at[pl.ds(0, n.nb - 1)])
    for phase, ref in (("cot", v.cot8), ("mix", v.mixs), ("grd", v.gs)):
        left(phase, ref.at[pl.ds(0, n.ng - 1)])
    left("hi", v.halo.at[1])
    left("lo", v.halo.at[0])
    left("ghi", v.ghalo.at[1])
    left("glo", v.ghalo.at[0])
    for k in range(n.kc):
        left(f"ra{k}", v.war.at[k])
        left(f"rb{k}", v.wbs.at[k, pl.ds(0, n.nx - 1)])
        left(f"rc{k}", v.wcs.at[k, pl.ds(0, n.nz - 1)])
        left(f"rd{k}", v.wdr.at[k, pl.ds(0, n.ng - 1)])
    left("re", v.wtot.at[0])
    left("fa", v.fas.at[pl.ds(0, n.nx - 1)])
    left("fb", v.fbr.at[pl.ds(0, 2 * n.nz - 1)])
    left("fc", v.fcr.at[pl.ds(0, n.nx - 1)])


class Sizes:
    pass


def shards(
    nx,
    field,
    cotangent,
    spec_weight,
    disco_coef,
    disco_weight,
    disco_rows,
    disco_shift,
    w_hidden,
    w_output,
):
    n = Sizes()
    _, n.cl, n.rows, n.lon = field.shape
    n.ne, n.nb, n.ng = (lax.axis_size(a) for a in ("ens", "lat", "chan"))
    n.nx = nx
    n.nz = n.nb // nx
    n.lat = n.rows * n.nb
    n.modes = n.lat // 2
    n.ml = n.modes // n.nb
    n.qn = 2 * n.ml
    n.deg = spec_weight.shape[1]
    n.ks = disco_coef.shape[1]
    n.chans, n.hid = w_hidden.shape
    n.frows = n.deg // n.nx
    n.kc = n.chans // LANES
    n.slot = 2 * (-(-(n.chans // n.nb) // 16) * 16)
    n.scale = 1.0 / math.sqrt(n.ne * n.lat * n.lon)
    plain, weighted, forward, inverse = constant_tables(n.lat, n.lon, n.modes, n.deg, n.nb)
    scratches = scratch(n)
    vmem = pl.BlockSpec(memory_space=pltpu.VMEM)
    smem = pl.BlockSpec(memory_space=pltpu.SMEM)
    hbm = pl.BlockSpec(memory_space=pl.ANY)
    share = n.chans // n.nb
    grad_field, grad_spec, grad_disco, grad_hidden, grad_output = pl.pallas_call(
        functools.partial(kernel, n, ARGS + tuple(scratches)),
        out_shape=(
            jax.ShapeDtypeStruct((n.cl, n.rows, n.lon), bf16),
            jax.ShapeDtypeStruct((2, n.cl, n.deg), f32),
            jax.ShapeDtypeStruct((n.ks, n.cl), f32),
            jax.ShapeDtypeStruct((share, n.hid), f32),
            jax.ShapeDtypeStruct((2 * share, n.chans), f32),
        ),
        in_specs=[vmem] * 8 + [smem] * 3 + [hbm] * 2,
        out_specs=(vmem,) * 5,
        scratch_shapes=list(scratches.values()),
        compiler_params=pltpu.CompilerParams(
            collective_id=0, has_side_effects=True, vmem_limit_bytes=56 * 1024 * 1024
        ),
    )(
        field[0],
        cotangent[0],
        jnp.transpose(spec_weight, (0, 2, 1)),
        disco_weight,
        w_hidden,
        w_output,
        jnp.asarray(forward),
        jnp.asarray(inverse),
        jnp.transpose(disco_coef),
        jnp.transpose(disco_rows),
        jnp.transpose(disco_shift),
        jnp.asarray(plain),
        jnp.asarray(weighted),
    )
    return (
        grad_field[None],
        jnp.transpose(grad_spec, (0, 2, 1)),
        grad_disco,
        grad_hidden,
        grad_output,
    )


def solution(mesh, nx=4):
    in_specs = (
        P("ens", "chan", "lat", None),
        P("ens", "chan", "lat", None),
        P(None, None, "chan"),
        P(),
        P(None, "chan"),
        P(),
        P(),
        P(),
        P(),
    )
    out_specs = (
        P("ens", "chan", "lat", None),
        P(None, None, "chan"),
        P(None, "chan"),
        P("lat", None),
        P("lat", None),
    )
    return jax.shard_map(
        functools.partial(shards, nx),
        mesh=mesh,
        in_specs=in_specs,
        out_specs=out_specs,
        check_vma=False,
    )
```

time: 487 us -> 72 us (0.15)
  the two profiles are of different devices: /device:TPU:256 before, /device:TPU:1 now
where the time goes in v1:
time: 72 us; the launch traced here: 71.8 us
  Pallas kernels  66.8 us (93%)
  local copies, waits for them, and re-layouts  4.26 us (6%)
    pallas_call x1, Pallas kernels, shards(): pl.pallas_call(functools.partial(kernel, n, ARGS + tuple(scratches)), out...  66.8 us
    unnamed x13, local copies, waits for them, and re-layouts  4.26 us

profile of v1, /device:TPU:1, one launch (start us, length us, event | category | flops | bytes accessed | tf_op | source)
XLA Modules:
  0.0 71.8 jit_solution(15327415720149168142)
XLA Ops:
  0.6 66.8 %shard_map.164 = (bf16[48,4,256]{2,1,0:T(4,128)(2,1)}, f32[2,48,64]{2,1,0:T(8,128)}, f32[9,48]{1,0:T(8,128)}, f32[12,768]{1,0:T(8,128)}, f32[24,384]{1,0:T(8,128)}) custom-call(bf16[48,4,256]{2,1,0:T(4,128)(2,1)} %bitcast.9, bf16[48,4,256]{2,1,0:T(4,128)(2,1)} %bitcast.10, f32[2,48,64]{2,1,0:T(8,128)} %bitcast.11, f32[9,48]{1,0:T(8,128)} %refs_3_.1, ...), custom_call_target="tpu_custom_call" | custom-call | tf_op jit(solution)/shard_map/pallas_call | solution.py:647
  67.5 0.0 copy-start.1
  67.5 1.6 %copy.23 = bf16[1,48,4,256]{3,2,1,0:T(4,128)(2,1)} copy(bf16[1,48,4,256]{3,2,1,0:T(4,128)(2,1)} %bitcast.8) | data formatting | bytes 196608
  69.1 0.0 copy-done.1
  69.1 0.0 copy-start.3
  69.1 0.0 copy-start
  69.1 0.6 copy.24
  69.7 0.1 copy-done.3
  69.8 0.6 copy.25
  70.4 0.0 copy-done
  70.4 0.0 copy-start.2
  70.4 0.6 copy.26
  71.0 0.1 copy-done.2
  71.1 0.6 copy.27
Async XLA Ops:
  67.5 1.6 %copy-start.1 = (f32[2,48,64]{2,1,0:T(8,128)S(1)}, f32[2,48,64]{2,1,0:T(8,128)}, u32[]{:S(2)}) copy-start(f32[2,48,64]{2,1,0:T(8,128)} %get-tuple-element.11) | copy-start | bytes 73732
  69.1 0.7 copy-start.3
  69.1 1.3 %copy-start = (f32[12,768]{1,0:T(8,128)S(1)}, f32[12,768]{1,0:T(8,128)}, u32[]{:S(2)}) copy-start(f32[12,768]{1,0:T(8,128)} %get-tuple-element.23) | copy-start | bytes 110596
  70.4 0.8 %copy-start.2 = (f32[24,384]{1,0:T(8,128)S(1)}, f32[24,384]{1,0:T(8,128)}, u32[]{:S(2)}) copy-start(f32[24,384]{1,0:T(8,128)} %get-tuple-element.24) | copy-start | bytes 110596

commit v2 on v1

--- a/solution.py
+++ b/solution.py
@@ -133,11 +133,11 @@
         wds=pltpu.VMEM((n.kc, n.slot, LANES), bf16),
         wdr=pltpu.VMEM((n.kc, n.ng, n.slot, LANES), bf16),
         wtot=pltpu.VMEM((2, n.kc, n.slot, LANES), f32),
-        fas=pltpu.VMEM((n.nx, 2 * n.frows, LANES), bf16),
-        far=pltpu.VMEM((n.nx, 2 * n.frows, LANES), bf16),
-        fbs=pltpu.VMEM((2 * n.frows, LANES), bf16),
-        fbr=pltpu.VMEM((2 * n.nz, 2 * n.frows, LANES), bf16),
-        fcr=pltpu.VMEM((n.nx, n.frows, LANES), f32),
+        fas=pltpu.VMEM((2 * n.nx, n.frows, LANES), bf16),
+        far=pltpu.VMEM((2 * n.nx, n.frows, LANES), bf16),
+        fbs=pltpu.VMEM((n.frows, LANES), bf16),
+        fbr=pltpu.VMEM((n.nz, n.frows, LANES), bf16),
+        fcr=pltpu.VMEM((2 * n.nx, n.frows, LANES), f32),
         load_sem=pltpu.SemaphoreType.DMA((2,)),
         send=pltpu.SemaphoreType.DMA((len(DMAS),)),
         recv=pltpu.SemaphoreType.DMA((len(DMAS),)),
@@ -210,12 +210,12 @@
         return carry
 
     def greet_ens(k, carry):
-        greet({"ens": 1 - me_e, "lat": k * n.nx + me_x})
+        greet({"ens": 1 - me_e, "lat": me_z * n.nx + k})
         return carry
 
     lax.fori_loop(0, n.nb - 1, greet_lat, 0)
     lax.fori_loop(1, n.ng, greet_chan, 0)
-    lax.fori_loop(0, n.nz, greet_ens, 0)
+    lax.fori_loop(0, n.nx, greet_ens, 0)
 
     load_p = pltpu.make_async_copy(v.p_hbm.at[me_b], v.pt, v.load_sem.at[0])
     load_q = pltpu.make_async_copy(v.q_hbm.at[me_b], v.qt, v.load_sem.at[1])
@@ -250,7 +250,7 @@
         row = v.wide[:, r, :].astype(bf16)
         v.cot8[2 * r] = row[:, :LANES]
         v.cot8[2 * r + 1] = row[:, LANES:]
-    pl.semaphore_wait(barrier, n.nb - 1 + n.ng - 1 + n.nz)
+    pl.semaphore_wait(barrier, n.nb - 1 + n.ng - 1 + n.nx)
 
     exchange("a1", "lat", me_b, n.nb, v.s1, v.r1)
     below, above = lat_peer(n.nb - 1), lat_peer(1)
@@ -439,8 +439,7 @@
 
     for k in range(n.kc):
         r_a(k)
-    for k in range(n.kc):
-        r_b(k)
+    r_b(0)
 
     arrived("grd", v.gr.at[pl.ds(0, n.ng - 1)])
     for r in range(n.rows):
@@ -449,6 +448,8 @@
     exchange("a5", "lat", me_b, n.nb, v.s5, v.r5)
     copy("ghi", v.gm.at[top], v.ghalo.at[1], {"lat": below}).start()
     copy("glo", v.gm.at[bottom], v.ghalo.at[0], {"lat": above}).start()
+    r_b(1)
+    r_b(2)
 
     lane = lax.broadcasted_iota(jnp.int32, (n.cl, LANES), 1)
 
@@ -492,7 +493,6 @@
         if r == n.rows // 2:
             r_c(0)
         spread(HALO + r, v.gm[r])
-    r_c(1)
 
     arrived("a5", v.r5.at[pl.ds(0, n.nb - 1)])
     grads = jnp.dot(v.pa[...], v.r5[...].reshape(total_rows, LANES), preferred_element_type=f32)
@@ -505,44 +505,46 @@
 
     real, imag = v.coeffs[:half, :], v.coeffs[half:, :]
     terms = (g_real * real + g_imag * imag, g_imag * real - g_real * imag)
-    parts = []
+    disco_part = pltpu.roll(v.dgrad[: n.frows, :], 64, 1)
+    low_lanes = lax.broadcasted_iota(jnp.int32, (n.frows, LANES), 1) < 64
     for t in range(2):
         part = terms[t][: n.deg]
         for m in range(1, n.ml):
             part = part + terms[t][m * n.deg : (m + 1) * n.deg]
-        parts.append(part)
-    low_lanes = lax.broadcasted_iota(jnp.int32, (n.deg, LANES), 1) < 64
-    both = jnp.where(low_lanes, parts[0], pltpu.roll(parts[1], 64, 1))
-    for x in range(n.nx):
-        v.fas[x, : n.frows, :] = both[x * n.frows : (x + 1) * n.frows].astype(bf16)
-        v.fas[x, n.frows :, :] = v.dgrad[: n.frows, :].astype(bf16)
+        for x in range(n.nx):
+            rows = part[x * n.frows : (x + 1) * n.frows]
+            v.fas[t * n.nx + x] = jnp.where(low_lanes, rows, disco_part).astype(bf16)
+    place = me_e * n.nx + me_x
+
+    def near(t):
+        p = lax.rem(place + t, 2 * n.nx)
+        return p, {"ens": lax.div(p, n.nx), "lat": me_z * n.nx + lax.rem(p, n.nx)}
 
     def send_fa(t, carry):
-        x = lax.rem(me_x + t, n.nx)
-        copy("fa", v.fas.at[x], v.far.at[me_x], {"lat": me_z * n.nx + x}).start()
+        p, to = near(t)
+        copy("fa", v.fas.at[p], v.far.at[place], to).start()
         return carry
 
-    lax.fori_loop(1, n.nx, send_fa, 0)
-    v.far[me_x] = v.fas[me_x]
-    r_c(2)
+    lax.fori_loop(1, 2 * n.nx, send_fa, 0)
+    v.far[place] = v.fas[place]
+    r_c(1)
 
     arrived("glo", v.ghalo.at[0])
     arrived("ghi", v.ghalo.at[1])
     spread(0, v.ghalo[0, 0])
     spread(1, v.ghalo[0, 1])
 
-    place = me_e * n.nz + me_z
-    arrived("fa", v.far.at[pl.ds(0, n.nx - 1)])
+    arrived("fa", v.far.at[pl.ds(0, 2 * n.nx - 1)])
     v.fbs[...] = jnp.sum(v.far[...].astype(f32), axis=0).astype(bf16)
 
     def send_fb(t, carry):
-        p = lax.rem(place + t, 2 * n.nz)
-        to = {"ens": lax.div(p, n.nz), "lat": lax.rem(p, n.nz) * n.nx + me_x}
-        copy("fb", v.fbs, v.fbr.at[place], to).start()
+        z = lax.rem(me_z + t, n.nz)
+        copy("fb", v.fbs, v.fbr.at[me_z], {"lat": z * n.nx + me_x}).start()
         return carry
 
-    lax.fori_loop(1, 2 * n.nz, send_fb, 0)
-    v.fbr[place] = v.fbs[...]
+    lax.fori_loop(1, n.nz, send_fb, 0)
+    v.fbr[me_z] = v.fbs[...]
+    r_c(2)
     r_d(0)
 
     spread(HALO + n.rows, v.ghalo[1, 0])
@@ -556,27 +558,26 @@
         v.wide[:, r, :] = base + row + v.back[r]
     v.gfield[...] = v.wide[...].astype(bf16)
 
-    arrived("fb", v.fbr.at[pl.ds(0, 2 * n.nz - 1)])
+    arrived("fb", v.fbr.at[pl.ds(0, n.nz - 1)])
     ftot = jnp.sum(v.fbr[...].astype(f32), axis=0)
-    v.fcr[me_x] = ftot[: n.frows]
+    v.fcr[place] = ftot
 
     def send_fc(t, carry):
-        x = lax.rem(me_x + t, n.nx)
-        copy("fc", v.fcr.at[me_x], v.fcr.at[me_x], {"lat": me_z * n.nx + x}).start()
+        p, to = near(t)
+        copy("fc", v.fcr.at[place], v.fcr.at[place], to).start()
         return carry
 
-    lax.fori_loop(1, n.nx, send_fc, 0)
-    v.gdw[...] = ftot[n.frows : n.frows + n.ks, : n.cl] * n.scale
+    lax.fori_loop(1, 2 * n.nx, send_fc, 0)
+    v.gdw[...] = pltpu.roll(ftot, 64, 1)[: n.ks, : n.cl] * n.scale
 
     for k in range(n.kc):
         r_e(k)
     copy("re", v.wtot.at[me_e], v.wtot.at[me_e], {"ens": 1 - me_e}).start()
 
-    arrived("fc", v.fcr.at[pl.ds(0, n.nx - 1)])
-    v.square[: n.deg, :] = v.fcr[...].reshape(n.deg, LANES)
-    flipped = jnp.transpose(v.square[...])
-    v.gsw[0] = flipped[: n.cl, : n.deg]
-    v.gsw[1] = flipped[64 : 64 + n.cl, : n.deg]
+    arrived("fc", v.fcr.at[pl.ds(0, 2 * n.nx - 1)])
+    flipped = jnp.transpose(v.fcr[...].reshape(2 * n.deg, LANES))
+    for t in range(2):
+        v.gsw[t] = flipped[: n.cl, t * n.deg : (t + 1) * n.deg]
 
     arrived("re", v.wtot.at[0])
     for k in range(n.kc):
@@ -601,13 +602,25 @@
         left(f"rc{k}", v.wcs.at[k, pl.ds(0, n.nz - 1)])
         left(f"rd{k}", v.wdr.at[k, pl.ds(0, n.ng - 1)])
     left("re", v.wtot.at[0])
-    left("fa", v.fas.at[pl.ds(0, n.nx - 1)])
-    left("fb", v.fbr.at[pl.ds(0, 2 * n.nz - 1)])
-    left("fc", v.fcr.at[pl.ds(0, n.nx - 1)])
+    left("fa", v.fas.at[pl.ds(0, 2 * n.nx - 1)])
+    left("fb", v.fbr.at[pl.ds(0, n.nz - 1)])
+    left("fc", v.fcr.at[pl.ds(0, 2 * n.nx - 1)])
 
 
 class Sizes:
     pass
+
+
+def copies(*refs):
+    count = len(refs) // 2
+    sems = refs[-1]
+    moves = [
+        pltpu.make_async_copy(refs[i], refs[count + i], sems.at[i]) for i in range(count)
+    ]
+    for move in moves:
+        move.start()
+    for move in moves:
+        move.wait()
 
 
 def shards(
@@ -644,15 +657,16 @@
     smem = pl.BlockSpec(memory_space=pltpu.SMEM)
     hbm = pl.BlockSpec(memory_space=pl.ANY)
     share = n.chans // n.nb
-    grad_field, grad_spec, grad_disco, grad_hidden, grad_output = pl.pallas_call(
+    shapes = (
+        jax.ShapeDtypeStruct((n.cl, n.rows, n.lon), bf16),
+        jax.ShapeDtypeStruct((2, n.cl, n.deg), f32),
+        jax.ShapeDtypeStruct((n.ks, n.cl), f32),
+        jax.ShapeDtypeStruct((share, n.hid), f32),
+        jax.ShapeDtypeStruct((2 * share, n.chans), f32),
+    )
+    results = pl.pallas_call(
         functools.partial(kernel, n, ARGS + tuple(scratches)),
-        out_shape=(
-            jax.ShapeDtypeStruct((n.cl, n.rows, n.lon), bf16),
-            jax.ShapeDtypeStruct((2, n.cl, n.deg), f32),
-            jax.ShapeDtypeStruct((n.ks, n.cl), f32),
-            jax.ShapeDtypeStruct((share, n.hid), f32),
-            jax.ShapeDtypeStruct((2 * share, n.chans), f32),
-        ),
+        out_shape=shapes,
         in_specs=[vmem] * 8 + [smem] * 3 + [hbm] * 2,
         out_specs=(vmem,) * 5,
         scratch_shapes=list(scratches.values()),
@@ -674,6 +688,13 @@
         jnp.asarray(plain),
         jnp.asarray(weighted),
     )
+    grad_field, grad_spec, grad_disco, grad_hidden, grad_output = pl.pallas_call(
+        copies,
+        out_shape=shapes,
+        in_specs=[hbm] * len(shapes),
+        out_specs=(hbm,) * len(shapes),
+        scratch_shapes=[pltpu.SemaphoreType.DMA((len(shapes),))],
+    )(*results)
     return (
         grad_field[None],
         jnp.transpose(grad_spec, (0, 2, 1)),

time: 72 us -> 76.5 us (1.062)
  Pallas kernels: 66.8 us -> 75.7 us
  local copies, waits for them, and re-layouts: 4.26 us -> 0 us
    pallas_call x0 -> x1, Pallas kernels: none -> 8.36 us  [shards(): pl.pallas_call(copies, out_shape=shapes, in_specs=[hbm] * len(shapes), ou...]
    unnamed x13 -> x0, local copies, waits for them, and re-layouts: 4.26 us -> none
where the time goes in v2:
time: 76.5 us; the launch traced here: 76.3 us
  Pallas kernels  75.7 us (99%)
    pallas_call x1, Pallas kernels, shards(): pl.pallas_call(functools.partial(kernel, n, ARGS + tuple(scratches)), out...  67.3 us
    pallas_call x1, Pallas kernels, shards(): pl.pallas_call(copies, out_shape=shapes, in_specs=[hbm] * len(shapes), ou...  8.36 us

profile of v2, /device:TPU:1, one launch (start us, length us, event | category | flops | bytes accessed | tf_op | source)
XLA Modules:
  0.0 76.3 jit_solution(13188406801394816904)
XLA Ops:
  0.6 67.3 %shard_map.164 = (bf16[48,4,256]{2,1,0:T(4,128)(2,1)}, f32[2,48,64]{2,1,0:T(8,128)}, f32[9,48]{1,0:T(8,128)}, f32[12,768]{1,0:T(8,128)}, f32[24,384]{1,0:T(8,128)}) custom-call(bf16[48,4,256]{2,1,0:T(4,128)(2,1)} %bitcast.8, bf16[48,4,256]{2,1,0:T(4,128)(2,1)} %bitcast.9, f32[2,48,64]{2,1,0:T(8,128)} %bitcast.10, f32[9,48]{1,0:T(8,128)} %refs_3_.1, ...), custom_call_target="tpu_custom_call" | custom-call | tf_op jit(solution)/shard_map/pallas_call | solution.py:667
  68.0 8.4 %shard_map.165 = (bf16[48,4,256]{2,1,0:T(4,128)(2,1)}, f32[2,48,64]{2,1,0:T(8,128)}, f32[9,48]{1,0:T(8,128)}, f32[12,768]{1,0:T(8,128)}, f32[24,384]{1,0:T(8,128)}) custom-call(bf16[48,4,256]{2,1,0:T(4,128)(2,1)} %get-tuple-element.15.refs_0_, f32[2,48,64]{2,1,0:T(8,128)} %get-tuple-element.16.refs_1_, f32[9,48]{1,0:T(8,128)} %get-tuple-element.17.refs_2_, ...), custom_call_target="tpu_custom_call" | custom-call | tf_op jit(solution)/shard_map/pallas_call | solution.py:691

commit v3 on v2

--- a/solution.py
+++ b/solution.py
@@ -171,6 +171,9 @@
     def lat_peer(k):
         return lax.rem(me_b + k, n.nb)
 
+    def farthest_first(t, count):
+        return count // 2 + jnp.where(lax.rem(t, 2) == 0, -lax.div(t, 2), lax.div(t + 1, 2))
+
     def lat_at(t):
         u = lax.div(t, n.nx)
         far = n.nz // 2
@@ -181,7 +184,7 @@
 
     def exchange(phase, axis, me, count, src, dst, whole=False):
         def step(k, carry):
-            d = lax.rem(me + k, count)
+            d = lax.rem(me + farthest_first(k, count), count)
             copy(phase, src if whole else src.at[d], dst.at[me], {axis: d}).start()
             return carry
 
@@ -191,9 +194,9 @@
             return carry
 
         if axis == "lat":
-            lax.fori_loop(0, count - 1, to_lat, 0)
+            lax.fori_loop(0, count - 1, to_lat, 0, unroll=True)
         else:
-            lax.fori_loop(1, count, step, 0)
+            lax.fori_loop(0, count - 1, step, 0)
         dst[me] = src[...] if whole else src[me]
 
     barrier = pltpu.get_barrier_semaphore()
@@ -321,7 +324,7 @@
             v.shifted[r * n.ks + k] = moved
             return total + (v.coef[k, first + r] * v.wcol[k]) * moved
 
-        v.disco[r] = lax.fori_loop(0, n.ks, tap, jnp.zeros((n.cl, n.lon), f32))
+        v.disco[r] = lax.fori_loop(0, n.ks, tap, jnp.zeros((n.cl, n.lon), f32), unroll=True)
 
     for t in range(2):
         mine = slice(t * half, (t + 1) * half)
@@ -461,7 +464,9 @@
             )
         return total + jnp.where(lane == k, jnp.sum(inner, axis=1, keepdims=True), 0.0)
 
-    weight_grad = lax.fori_loop(0, n.ks, weight_tap, jnp.zeros((n.cl, LANES), f32))
+    weight_grad = lax.fori_loop(
+        0, n.ks, weight_tap, jnp.zeros((n.cl, LANES), f32), unroll=True
+    )
     v.square[...] = jnp.zeros((LANES, LANES), f32)
     v.square[: n.cl, :] = weight_grad
     v.dgrad[...] = jnp.transpose(v.square[...])
@@ -486,7 +491,7 @@
             )
 
         start = tuple(v.back[r] for r in targets)
-        for r, total in zip(targets, lax.fori_loop(0, n.ks, tap, start)):
+        for r, total in zip(targets, lax.fori_loop(0, n.ks, tap, start, unroll=True)):
             v.back[r] = total
 
     for r in range(n.rows):
@@ -499,10 +504,6 @@
     g_real, g_imag = grads[:half], grads[half:]
     s0, s1 = v.sww[0], v.sww[1]
     g_coeffs = jnp.concatenate([s0 * g_real + s1 * g_imag, s0 * g_imag - s1 * g_real], axis=0)
-    back_spec = jnp.dot(v.qb[...], g_coeffs.astype(bf16), preferred_element_type=f32)
-    v.s6[...] = back_spec.astype(bf16).reshape(n.nb, piece, LANES)
-    exchange("a6", "lat", me_b, n.nb, v.s6, v.r6)
-
     real, imag = v.coeffs[:half, :], v.coeffs[half:, :]
     terms = (g_real * real + g_imag * imag, g_imag * real - g_real * imag)
     disco_part = pltpu.roll(v.dgrad[: n.frows, :], 64, 1)
@@ -527,6 +528,9 @@
 
     lax.fori_loop(1, 2 * n.nx, send_fa, 0)
     v.far[place] = v.fas[place]
+    back_spec = jnp.dot(v.qb[...], g_coeffs.astype(bf16), preferred_element_type=f32)
+    v.s6[...] = back_spec.astype(bf16).reshape(n.nb, piece, LANES)
+    exchange("a6", "lat", me_b, n.nb, v.s6, v.r6)
     r_c(1)
 
     arrived("glo", v.ghalo.at[0])
@@ -550,7 +554,6 @@
     spread(HALO + n.rows, v.ghalo[1, 0])
     spread(HALO + n.rows + 1, v.ghalo[1, 1])
     r_d(1)
-    r_d(2)
 
     arrived("a6", v.r6.at[pl.ds(0, n.nb - 1)])
     for r, row in enumerate(from_pieces(v.fwd, v.r6)):
@@ -570,6 +573,7 @@
     lax.fori_loop(1, 2 * n.nx, send_fc, 0)
     v.gdw[...] = pltpu.roll(ftot, 64, 1)[: n.ks, : n.cl] * n.scale
 
+    r_d(2)
     for k in range(n.kc):
         r_e(k)
     copy("re", v.wtot.at[me_e], v.wtot.at[me_e], {"ens": 1 - me_e}).start()
@@ -613,14 +617,8 @@
 
 def copies(*refs):
     count = len(refs) // 2
-    sems = refs[-1]
-    moves = [
-        pltpu.make_async_copy(refs[i], refs[count + i], sems.at[i]) for i in range(count)
-    ]
-    for move in moves:
-        move.start()
-    for move in moves:
-        move.wait()
+    for source, target in zip(refs[:count], refs[count:]):
+        target[...] = source[...]
 
 
 def shards(
@@ -691,9 +689,8 @@
     grad_field, grad_spec, grad_disco, grad_hidden, grad_output = pl.pallas_call(
         copies,
         out_shape=shapes,
-        in_specs=[hbm] * len(shapes),
-        out_specs=(hbm,) * len(shapes),
-        scratch_shapes=[pltpu.SemaphoreType.DMA((len(shapes),))],
+        in_specs=[vmem] * len(shapes),
+        out_specs=(vmem,) * len(shapes),
     )(*results)
     return (
         grad_field[None],

time: 76.5 us -> 67.2 us (0.88)
  Pallas kernels: 75.7 us -> 66.4 us
    pallas_call x1, Pallas kernels: 8.36 us -> 1.65 us  [shards(): pl.pallas_call(copies, out_shape=shapes, in_specs=[vmem] * len(shapes), o...]
    pallas_call x1, Pallas kernels: 67.3 us -> 64.8 us  [shards(): pl.pallas_call(functools.partial(kernel, n, ARGS + tuple(scratches)), out...]
where the time goes in v3:
time: 67.2 us; the launch traced here: 67 us
  Pallas kernels  66.4 us (99%)
    pallas_call x1, Pallas kernels, shards(): pl.pallas_call(functools.partial(kernel, n, ARGS + tuple(scratches)), out...  64.8 us
    pallas_call x1, Pallas kernels, shards(): pl.pallas_call(copies, out_shape=shapes, in_specs=[vmem] * len(shapes), o...  1.65 us

profile of v3, /device:TPU:1, one launch (start us, length us, event | category | flops | bytes accessed | tf_op | source)
XLA Modules:
  0.0 67.0 jit_solution(904796925981510925)
XLA Ops:
  0.6 64.8 %shard_map.164 = (bf16[48,4,256]{2,1,0:T(4,128)(2,1)}, f32[2,48,64]{2,1,0:T(8,128)}, f32[9,48]{1,0:T(8,128)}, f32[12,768]{1,0:T(8,128)}, f32[24,384]{1,0:T(8,128)}) custom-call(bf16[48,4,256]{2,1,0:T(4,128)(2,1)} %bitcast.8, bf16[48,4,256]{2,1,0:T(4,128)(2,1)} %bitcast.9, f32[2,48,64]{2,1,0:T(8,128)} %bitcast.10, f32[9,48]{1,0:T(8,128)} %refs_3_.1, ...), custom_call_target="tpu_custom_call" | custom-call | tf_op jit(solution)/shard_map/pallas_call | solution.py:665
  65.4 1.6 %shard_map.165 = (bf16[48,4,256]{2,1,0:T(4,128)(2,1)}, f32[2,48,64]{2,1,0:T(8,128)}, f32[9,48]{1,0:T(8,128)}, f32[12,768]{1,0:T(8,128)}, f32[24,384]{1,0:T(8,128)}) custom-call(bf16[48,4,256]{2,1,0:T(4,128)(2,1)} %get-tuple-element.15.refs_0_, f32[2,48,64]{2,1,0:T(8,128)} %get-tuple-element.16.refs_1_, f32[9,48]{1,0:T(8,128)} %get-tuple-element.17.refs_2_, ...), custom_call_target="tpu_custom_call" | custom-call | tf_op jit(solution)/shard_map/pallas_call | solution.py:689

commit v4 on v3

--- a/solution.py
+++ b/solution.py
@@ -122,10 +122,14 @@
         n32=pltpu.VMEM((n.chans, LANES), f32),
         np32=pltpu.VMEM((n.chans, LANES), f32),
         ap32=pltpu.VMEM((n.hid, LANES), f32),
-        was=pltpu.VMEM((2, n.kc, n.nx, n.hid // n.nx, LANES), bf16),
-        war=pltpu.VMEM((n.kc, n.nx, n.hid // n.nx, LANES), bf16),
-        wbs=pltpu.VMEM((n.kc, n.nx, n.hid // n.nx, LANES), bf16),
-        wbr=pltpu.VMEM((n.kc, n.nx, n.hid // n.nx, LANES), bf16),
+        was=pltpu.VMEM((2, n.kc - 1, n.nx, n.hid // n.nx, LANES), bf16),
+        war=pltpu.VMEM((n.kc - 1, n.nx, n.hid // n.nx, LANES), bf16),
+        wbs=pltpu.VMEM((n.kc - 1, n.nx, n.hid // n.nx, LANES), bf16),
+        wbr=pltpu.VMEM((n.kc - 1, n.nx, n.hid // n.nx, LANES), bf16),
+        zas=pltpu.VMEM((2, n.nz, n.hid // n.nz, LANES), bf16),
+        zar=pltpu.VMEM((n.nz, n.hid // n.nz, LANES), bf16),
+        zbs=pltpu.VMEM((n.nz, n.hid // n.nz, LANES), bf16),
+        zbr=pltpu.VMEM((n.nz, n.hid // n.nz, LANES), bf16),
         wsum=pltpu.VMEM((n.hid // n.nx, LANES), f32),
         wslot=pltpu.VMEM((n.nz, n.slot, LANES), f32),
         wcs=pltpu.VMEM((n.kc, n.nz, n.slot, LANES), bf16),
@@ -366,67 +370,87 @@
             at, to = (z * n.nx + x) * share, (x * n.nz + z) * share
             v.np32[to : to + share, :] = v.n32[at : at + share, :]
             v.ap32[2 * to : 2 * (to + share), :] = activated[2 * at : 2 * (at + share)]
-    normed = v.np32[...].astype(bf16)
-    activated = v.ap32[...].astype(bf16)
+    plain = (v.n32[...].astype(bf16), activated.astype(bf16))
+    sorted_rows = (v.np32[...].astype(bf16), v.ap32[...].astype(bf16))
     adjoint = v.cotall[...].reshape(n.chans, LANES)
-    cols, depth = n.chans // n.nx, n.hid // n.nx
+    last = n.kc - 1
+
+    def path(k):
+        along_x = (n.nx, me_x, lambda x: {"lat": me_z * n.nx + x})
+        along_z = (n.nz, me_z, lambda z: {"lat": z * n.nx + me_x})
+        return (along_z, along_x) if k == last else (along_x, along_z)
+
+    def first_refs(k):
+        if k == last:
+            return v.zas, v.zar, v.zbs, v.zbr
+        return v.was.at[:, k], v.war.at[k], v.wbs.at[k], v.wbr.at[k]
 
     def r_a(k):
+        count = path(k)[0][0]
+        cols, depth = n.chans // count, n.hid // count
+        normed, active = plain if k == last else sorted_rows
+        mine, other, _, _ = first_refs(k)
         for half in range(2):
             at = half * n.chans + k * LANES
             hidden = lax.dot_general(
                 normed, v.gpre[at : at + LANES, :], NT, preferred_element_type=f32
             ).astype(bf16)
-            for x in range(n.nx):
-                rows = hidden[x * cols : (x + 1) * cols]
-                v.was[0, k, x, half * cols : (half + 1) * cols, :] = rows
+            for p in range(count):
+                rows = hidden[p * cols : (p + 1) * cols]
+                mine[0, p, half * cols : (half + 1) * cols, :] = rows
         output = lax.dot_general(
-            activated, adjoint[k * LANES : (k + 1) * LANES], NT, preferred_element_type=f32
+            active, adjoint[k * LANES : (k + 1) * LANES], NT, preferred_element_type=f32
         )
-        v.was[1, k] = output.astype(bf16).reshape(n.nx, depth, LANES)
-        copy(f"ra{k}", v.was.at[1 - me_e, k], v.war.at[k], {"ens": 1 - me_e}).start()
+        mine[1] = output.astype(bf16).reshape(count, depth, LANES)
+        copy(f"ra{k}", mine.at[1 - me_e], other, {"ens": 1 - me_e}).start()
 
     def r_b(k):
-        arrived(f"ra{k}", v.war.at[k])
-        v.wbs[k] = (v.was[me_e, k].astype(f32) + v.war[k].astype(f32)).astype(bf16)
+        count, place, device = path(k)[0]
+        mine, other, out, into = first_refs(k)
+        arrived(f"ra{k}", other)
+        out[...] = (mine[me_e].astype(f32) + other[...].astype(f32)).astype(bf16)
 
         def send(t, carry):
-            x = lax.rem(me_x + t, n.nx)
-            copy(f"rb{k}", v.wbs.at[k, x], v.wbr.at[k, me_x], {"lat": me_z * n.nx + x}).start()
+            p = lax.rem(place + farthest_first(t, count), count)
+            copy(f"rb{k}", out.at[p], into.at[place], device(p)).start()
             return carry
 
-        lax.fori_loop(1, n.nx, send, 0)
-        v.wbr[k, me_x] = v.wbs[k, me_x]
+        lax.fori_loop(0, count - 1, send, 0)
+        into[place] = out[place]
 
     def r_c(k):
-        arrived(f"rb{k}", v.wbr.at[k, pl.ds(0, n.nx - 1)])
-        v.wsum[...] = jnp.sum(v.wbr[k].astype(f32), axis=0)
+        (count, _, _), (owners, place, device) = path(k)
+        into = first_refs(k)[3]
+        cols, depth = n.chans // count, n.hid // count
+        arrived(f"rb{k}", into.at[pl.ds(0, count - 1)])
+        v.wsum[:depth, :] = jnp.sum(into[...].astype(f32), axis=0)
 
         @pl.when(me_e == 0)
         def _():
-            for z in range(n.nz):
+            for p in range(owners):
                 for half in range(2):
-                    at, to = half * cols + z * share, half * (n.slot // 2)
-                    v.wslot[z, to : to + share, :] = v.wsum[at : at + share, :]
+                    at, to = half * cols + p * share, half * (n.slot // 2)
+                    v.wslot[p, to : to + share, :] = v.wsum[at : at + share, :]
 
         @pl.when(me_e == 1)
         def _():
-            for z in range(n.nz):
-                v.wslot[z, : 2 * share, :] = v.wsum[2 * z * share : 2 * (z + 1) * share, :]
-
-        v.wcs[k] = v.wslot[...].astype(bf16)
+            for p in range(owners):
+                v.wslot[p, : 2 * share, :] = v.wsum[2 * p * share : 2 * (p + 1) * share, :]
+
+        v.wcs[k, :owners] = v.wslot[:owners].astype(bf16)
 
         def send(t, carry):
-            z = lax.rem(me_z + t, n.nz)
-            copy(f"rc{k}", v.wcs.at[k, z], v.wcr.at[k, me_z], {"lat": z * n.nx + me_x}).start()
+            p = lax.rem(place + farthest_first(t, owners), owners)
+            copy(f"rc{k}", v.wcs.at[k, p], v.wcr.at[k, place], device(p)).start()
             return carry
 
-        lax.fori_loop(1, n.nz, send, 0)
-        v.wcr[k, me_z] = v.wcs[k, me_z]
+        lax.fori_loop(0, owners - 1, send, 0)
+        v.wcr[k, place] = v.wcs[k, place]
 
     def r_d(k):
-        arrived(f"rc{k}", v.wcr.at[k, pl.ds(0, n.nz - 1)])
-        v.wds[k] = jnp.sum(v.wcr[k].astype(f32), axis=0).astype(bf16)
+        owners = path(k)[1][0]
+        arrived(f"rc{k}", v.wcr.at[k, pl.ds(0, owners - 1)])
+        v.wds[k] = jnp.sum(v.wcr[k, :owners].astype(f32), axis=0).astype(bf16)
 
         def send(t, carry):
             g = lax.rem(me_g + t, n.ng)
@@ -538,6 +562,7 @@
     spread(0, v.ghalo[0, 0])
     spread(1, v.ghalo[0, 1])
 
+    r_c(2)
     arrived("fa", v.far.at[pl.ds(0, 2 * n.nx - 1)])
     v.fbs[...] = jnp.sum(v.far[...].astype(f32), axis=0).astype(bf16)
 
@@ -548,12 +573,13 @@
 
     lax.fori_loop(1, n.nz, send_fb, 0)
     v.fbr[me_z] = v.fbs[...]
-    r_c(2)
     r_d(0)
 
     spread(HALO + n.rows, v.ghalo[1, 0])
     spread(HALO + n.rows + 1, v.ghalo[1, 1])
     r_d(1)
+
+    r_d(2)
 
     arrived("a6", v.r6.at[pl.ds(0, n.nb - 1)])
     for r, row in enumerate(from_pieces(v.fwd, v.r6)):
@@ -573,7 +599,6 @@
     lax.fori_loop(1, 2 * n.nx, send_fc, 0)
     v.gdw[...] = pltpu.roll(ftot, 64, 1)[: n.ks, : n.cl] * n.scale
 
-    r_d(2)
     for k in range(n.kc):
         r_e(k)
     copy("re", v.wtot.at[me_e], v.wtot.at[me_e], {"ens": 1 - me_e}).start()
@@ -601,9 +626,11 @@
     left("ghi", v.ghalo.at[1])
     left("glo", v.ghalo.at[0])
     for k in range(n.kc):
-        left(f"ra{k}", v.war.at[k])
-        left(f"rb{k}", v.wbs.at[k, pl.ds(0, n.nx - 1)])
-        left(f"rc{k}", v.wcs.at[k, pl.ds(0, n.nz - 1)])
+        (count, _, _), (owners, _, _) = path(k)
+        _, other, out, _ = first_refs(k)
+        left(f"ra{k}", other)
+        left(f"rb{k}", out.at[pl.ds(0, count - 1)])
+        left(f"rc{k}", v.wcs.at[k, pl.ds(0, owners - 1)])
         left(f"rd{k}", v.wdr.at[k, pl.ds(0, n.ng - 1)])
     left("re", v.wtot.at[0])
     left("fa", v.fas.at[pl.ds(0, 2 * n.nx - 1)])

time: 67.2 us -> 65.4 us (0.973)
  Pallas kernels: 66.4 us -> 64.6 us
    pallas_call x1, Pallas kernels: 64.8 us -> 62.9 us  [shards(): pl.pallas_call(functools.partial(kernel, n, ARGS + tuple(scratches)), out...]
where the time goes in v4:
time: 65.4 us; the launch traced here: 65.2 us
  Pallas kernels  64.6 us (99%)
    pallas_call x1, Pallas kernels, shards(): pl.pallas_call(functools.partial(kernel, n, ARGS + tuple(scratches)), out...  62.9 us
    pallas_call x1, Pallas kernels, shards(): pl.pallas_call(copies, out_shape=shapes, in_specs=[vmem] * len(shapes), o...  1.65 us

profile of v4, /device:TPU:1, one launch (start us, length us, event | category | flops | bytes accessed | tf_op | source)
XLA Modules:
  0.0 65.2 jit_solution(3917629576475682488)
XLA Ops:
  0.6 62.9 %shard_map.164 = (bf16[48,4,256]{2,1,0:T(4,128)(2,1)}, f32[2,48,64]{2,1,0:T(8,128)}, f32[9,48]{1,0:T(8,128)}, f32[12,768]{1,0:T(8,128)}, f32[24,384]{1,0:T(8,128)}) custom-call(bf16[48,4,256]{2,1,0:T(4,128)(2,1)} %bitcast.8, bf16[48,4,256]{2,1,0:T(4,128)(2,1)} %bitcast.9, f32[2,48,64]{2,1,0:T(8,128)} %bitcast.10, f32[9,48]{1,0:T(8,128)} %refs_3_.1, ...), custom_call_target="tpu_custom_call" | custom-call | tf_op jit(solution)/shard_map/pallas_call | solution.py:692
  63.6 1.6 %shard_map.165 = (bf16[48,4,256]{2,1,0:T(4,128)(2,1)}, f32[2,48,64]{2,1,0:T(8,128)}, f32[9,48]{1,0:T(8,128)}, f32[12,768]{1,0:T(8,128)}, f32[24,384]{1,0:T(8,128)}) custom-call(bf16[48,4,256]{2,1,0:T(4,128)(2,1)} %get-tuple-element.15.refs_0_, f32[2,48,64]{2,1,0:T(8,128)} %get-tuple-element.16.refs_1_, f32[9,48]{1,0:T(8,128)} %get-tuple-element.17.refs_2_, ...), custom_call_target="tpu_custom_call" | custom-call | tf_op jit(solution)/shard_map/pallas_call | solution.py:716
